TPU v7x, 128 devices: a whole 4x4x4 slice. The times are simulated.
128 devices in a mesh: dp: 32 (over y, z_lo, x), group: 4 (over z_hi, core).
Axes of the slice: x: 4, y: 4, z: 4 (z_hi: 2, z_lo: 2; z = z_hi * 2 + z_lo), core: 2. Of those that a mesh axis runs over, the one named last changes fastest.
Arguments:
- tokens: bfloat16 [2, 32, 1024, 1024], P(None, 'dp', 'group'), may hold values from -6 to 6
- segments: int32 [2, 32, 1024], P(None, 'dp'), may hold values from 0 to 1023, as said below
- cotangent: bfloat16 [2, 32, 1024, 1024], P(None, 'dp', 'group'), may hold values from -6 to 6
- norm_gain: bfloat16 [1024], replicated, may hold values from 0.5 to 1.5
- in_weight: bfloat16 [1024, 4384], replicated, may hold values from -0.1875 to 0.1875
- conv_kernel: bfloat16 [4, 2304], replicated, may hold values from -3 to 3
- conv_bias: bfloat16 [2304], replicated, may hold values from -0.5 to 0.5
- step_bias: bfloat16 [32], replicated, may hold values from -6.5 to -2.5
- decay_log: bfloat16 [32], replicated, may hold values from 0 to 2.796875
- skip_gain: bfloat16 [32], replicated, may hold values from 0.5 to 1.5
- gate_gain: bfloat16 [2048], replicated, may hold values from 0.5 to 1.5
- out_weight: bfloat16 [2048, 1024], replicated, may hold values from -0.125 to 0.125
- master: float32 [6602752], P('dp'), may hold values from -0.75 to 0.75
- moment_one: float32 [6602752], P('dp'), may hold values from -0.00390625 to 0.00390625
- moment_two: float32 [6602752], P('dp'), may hold values from 1e-08 to 1e-06
- step_count: int32 [1], replicated, may hold values from 1 to 8
Outputs:
- output: bfloat16 [2, 32, 1024, 1024], P(None, 'dp', 'group')
- input_grad: bfloat16 [2, 32, 1024, 1024], P(None, 'dp', 'group')
- flat_grad: float32 [6602752], P('dp')
- moment_one_new: float32 [6602752], P('dp')
- moment_two_new: float32 [6602752], P('dp')
- master_new: float32 [6602752], P('dp')
- weights_copy: bfloat16 [6602752], replicated
Inputs may be any that keep to these rules, and one draw needn't show every extreme that they name: `segments`: within each sequence the numbers start at 0, never fall and rise by at most one from a token to the next; of every 4 consecutive sequences of a micro-batch (sequences 0 to 3, 4 to 7 and so on) one is a single document; in every micro-batch one of sequences 0 to 3 starts a new document at every token.
All inputs are finite; a program needn't handle non-finite values.
Results may differ from a plain program's by a relative error of at most 0.0067.
Values may be sent and summed in bfloat16 or wider, within the bound.
No kernel may reach another device: no remote copies, remote signals or barrier semaphores. Data moves between devices by JAX's collectives and lax.ppermute only.
A program may use at most 256 MiB of HBM per device.

v0:
```python
import jax
import jax.numpy as jnp
from jax import lax
from jax.sharding import Mesh
from jax.sharding import PartitionSpec as P

D = 1024
DI = 2048
HEADS = 32
HDIM = 64
STATE = 128
KCONV = 4
CH = 2304
NPARAM = 6601056
DP = ("dp_0", "dp_1", "dp_2")
DP_GROUP = ("dp_0", "dp_1", "dp_2", "group")


EPSILON = 1e-05
BETA_ONE = 0.9
BETA_TWO = 0.95
ADAM_EPSILON = 1e-08
LEARN_RATE = 0.01
WEIGHT_DECAY = 0.1
MAX_NORM = 1.0
HIGHEST_PRECISION = lax.Precision.HIGHEST


def from_behind(block, axis, distance):
    devices = range(lax.axis_size(axis))
    route = [(i - distance, i) for i in devices if i - distance in devices]
    return lax.ppermute(block, axis, route)


def carried_in(value, axis, join, neutral, backward):
    count, mine = (lax.axis_size(axis), lax.axis_index(axis))
    pieces = jax.tree.map(lambda part: lax.all_gather(part, axis), value)
    if backward:
        pieces = jax.tree.map(lambda part: part[::-1], pieces)
        mine = count - 1 - mine
    running = jax.tree.map(
        lambda part, zero: jnp.full_like(part, 0) + jnp.asarray(zero, part.dtype), value, neutral
    )

    def step(position, running):
        longer = join(running, jax.tree.map(lambda part: part[position], pieces))
        return jax.tree.map(lambda new, old: jnp.where(position < mine, new, old), longer, running)

    return lax.fori_loop(0, count - 1, step, running)


def split_up(shard, dim, size):
    lengths = shard.shape
    parts = shard.reshape(*lengths[:dim], size, lengths[dim] // size, *lengths[dim + 1 :])
    return jnp.moveaxis(parts, dim, 0)


def sum_in_tiles(shard, axis, dim):
    size = lax.axis_size(axis)
    parts = split_up(shard, dim, size)
    lines = parts.reshape(size, -1)
    extent = max(16, -(-lines.shape[1] // 1024) * 8)
    lines = jnp.pad(lines, ((0, 0), (0, extent * 128 - lines.shape[1]))).reshape(-1, 128)
    own = lax.psum_scatter(lines, axis, scatter_dimension=0, tiled=True)
    return own.reshape(-1)[: parts[0].size].reshape(parts.shape[1:])


def laid_out(parts, dim):
    parts = jnp.moveaxis(parts, 0, dim)
    lengths = parts.shape
    return parts.reshape(*lengths[:dim], lengths[dim] * lengths[dim + 1], *lengths[dim + 2 :])


def sent_to_all(shard, axis):
    copies = jnp.broadcast_to(shard, (lax.axis_size(axis), *shard.shape))
    return lax.all_to_all(copies, axis, split_axis=0, concat_axis=0, tiled=True)


def collect(shard, axis, dim):
    return laid_out(sent_to_all(shard, axis), dim)


def over_copies(shard, axis):
    everything = sent_to_all(shard, axis)
    return jnp.sum(everything, axis=0)


def edges_of(length, count):
    unit = 8 if length >= 8 * count else 1
    return [length // unit * k // count * unit for k in range(1, count)]


def gather_in_order(shard, axes, sequence):
    parts = shard[None]
    for k in sequence:
        parts = lax.all_gather(parts, axes[k], axis=0, tiled=True)
    block = [lax.axis_size(axes[k]) for k in reversed(sequence)]
    parts = parts.reshape(*block, *shard.shape)
    turned = sorted(range(len(sequence)), key=lambda place: sequence[len(sequence) - 1 - place])
    return parts.transpose(*turned, *range(len(sequence), parts.ndim)).reshape(-1, *shard.shape)


def spread_gather(shard, axes, dim):
    numbers = list(range(len(axes)))[::-1]
    widest = shard.shape.index(max(shard.shape[:-1] or shard.shape))
    edges = [0, *edges_of(shard.shape[widest], len(axes)), shard.shape[widest]]
    outs = []
    for k, (start, end) in enumerate(zip(edges, edges[1:])):
        if end > start:
            slab = lax.slice_in_dim(shard, start, end, axis=widest)
            outs.append(gather_in_order(slab, axes, numbers[k:] + numbers[:k]))
    return laid_out(jnp.concatenate(outs, axis=widest + 1), dim)


def norm_piece(values, scaling):
    factor = lax.rsqrt(jnp.mean(values * values, axis=-1, keepdims=True) + EPSILON)
    return values * factor * scaling


def prepare(padded, raw_steps, kernel, shift_bias, step_shift, decay_rate, tap_mask):
    length = raw_steps.shape[0]
    summed = shift_bias + tap_mask[0][:, None] * padded[0:length] * kernel[0]
    for offset in range(1, kernel.shape[0]):
        summed = (
            summed + tap_mask[offset][:, None] * padded[offset : offset + length] * kernel[offset]
        )
    active = jax.nn.silu(summed)
    signal = active[:, :DI]
    write_map = active[:, DI : DI + STATE]
    read_map = active[:, DI + STATE :]
    step_size = jax.nn.softplus(raw_steps + step_shift)
    log_decay = -step_size * jnp.exp(decay_rate)
    inflow = (signal * jnp.repeat(step_size, HDIM, axis=1)).reshape(length, HEADS, HDIM)
    return (signal, inflow, write_map, read_map, log_decay)


def doc_masks(doc_ids, prior_id):
    places = jnp.arange(doc_ids.shape[0])
    same_doc = (
        (doc_ids[:, None] == doc_ids[None, :]) & (places[:, None] >= places[None, :])
    ).astype(jnp.float32)
    carry_mask = (doc_ids == prior_id).astype(jnp.float32)
    end_mask = (doc_ids == doc_ids[-1]).astype(jnp.float32)
    total_mask = (doc_ids[-1] == prior_id).astype(jnp.float32)
    return (same_doc, carry_mask, end_mask, total_mask)


def mix_out(
    signal,
    inflow,
    write_map,
    read_map,
    cum_decay,
    state_in,
    gate_z,
    skip_gain,
    gate_gain,
    same_doc,
    carry_mask,
):
    spread = cum_decay[:, None, :] - cum_decay[None, :, :]
    inside = same_doc[:, :, None] > 0
    kernel = jnp.where(inside, jnp.exp(jnp.where(inside, spread, 0.0)), 0.0)
    intersection = jnp.dot(read_map, write_map.T, precision=HIGHEST_PRECISION)
    within = jnp.einsum(
        "ijh,ij,jhp->ihp", kernel, intersection, inflow, precision=HIGHEST_PRECISION
    )
    entry = carry_mask[:, None] * jnp.exp(cum_decay)
    carried = (
        jnp.einsum("is,hps->ihp", read_map, state_in, precision=HIGHEST_PRECISION)
        * entry[:, :, None]
    )
    scanned = (within + carried).reshape(signal.shape) + signal * jnp.repeat(skip_gain, HDIM)
    gated = scanned * jax.nn.silu(gate_z)
    factor = lax.rsqrt(jnp.mean(gated * gated, axis=-1, keepdims=True) + EPSILON)
    return gated * factor * gate_gain


def mix_state(inflow, write_map, cum_decay, end_mask, total_mask):
    tail_weight = end_mask[:, None] * jnp.exp(cum_decay[-1][None, :] - cum_decay)
    local_state = jnp.einsum(
        "jh,jhp,js->hps", tail_weight, inflow, write_map, precision=HIGHEST_PRECISION
    )
    through = total_mask * jnp.exp(cum_decay[-1])
    return (through, local_state)


def adam_update(clipped, master, moment_one, moment_two, step_count):
    first_moment = BETA_ONE * moment_one + (1.0 - BETA_ONE) * clipped
    second_moment = BETA_TWO * moment_two + (1.0 - BETA_TWO) * clipped * clipped
    step_real = step_count[0].astype(jnp.float32)
    first_hat = first_moment / (1.0 - jnp.power(BETA_ONE, step_real))
    second_hat = second_moment / (1.0 - jnp.power(BETA_TWO, step_real))
    updated = master - LEARN_RATE * (
        first_hat / (jnp.sqrt(second_hat) + ADAM_EPSILON) + WEIGHT_DECAY * master
    )
    return (first_moment, second_moment, updated)


def chain(earlier, later):
    first_decay, first_state = earlier
    second_decay, second_state = later
    return (first_decay * second_decay, second_decay[:, :, None, None] * first_state + second_state)


def back_chain(earlier, later):
    upper_decay, upper_grad = earlier
    lower_decay, lower_grad = later
    return (upper_decay * lower_decay, lower_grad + lower_decay[:, :, None, None] * upper_grad)


def contract_rows(left, right):
    return lax.dot_general(
        left, right, (((0,), (0,)), ((), ())), preferred_element_type=jnp.float32
    )


def contract_cols(left, right):
    return lax.dot_general(
        left, right, (((1,), (1,)), ((), ())), preferred_element_type=jnp.float32
    )


def shards(
    tokens,
    segments,
    cotangent,
    norm_gain,
    in_weight,
    conv_kernel,
    conv_bias,
    step_bias,
    decay_log,
    skip_gain,
    gate_gain,
    out_weight,
    master,
    moment_one,
    moment_two,
    step_count,
):
    micro_count = tokens.shape[0]
    seq_count = tokens.shape[1]
    span_len = tokens.shape[2]
    rim_width = KCONV - 1
    norm_real = norm_gain.astype(jnp.float32)
    kernel_real = conv_kernel.astype(jnp.float32)
    shifts_real = conv_bias.astype(jnp.float32)
    steps_real = step_bias.astype(jnp.float32)
    decays_real = decay_log.astype(jnp.float32)
    skips_real = skip_gain.astype(jnp.float32)
    gains_real = gate_gain.astype(jnp.float32)
    group_place = lax.axis_index("group")
    filler = jnp.full((seq_count, rim_width), -1, jnp.int32)
    outputs = []
    input_grads = []
    totals = None
    for batch_index in range(micro_count):
        seg_window = lax.dynamic_slice_in_dim(
            jnp.concatenate([filler, segments[batch_index]], axis=1),
            group_place * span_len,
            span_len + rim_width,
            axis=1,
        )
        doc_ids = seg_window[:, rim_width:]
        prior_ids = seg_window[:, rim_width - 1]
        tap_mask = jnp.stack(
            [seg_window[:, offset : offset + span_len] == doc_ids for offset in range(KCONV)],
            axis=1,
        ).astype(jnp.float32)
        same_doc, carry_mask, end_mask, total_mask = jax.vmap(doc_masks)(doc_ids, prior_ids)
        rows_in = tokens[batch_index].reshape(-1, D).astype(jnp.float32)
        normed, norm_back = jax.vjp(norm_piece, rows_in, norm_real)
        normed_low = normed.astype(jnp.bfloat16)
        projected = jnp.dot(normed_low, in_weight, preferred_element_type=jnp.float32)
        gate_z = projected[:, :DI].reshape(seq_count, span_len, DI)
        conv_input = (
            projected[:, DI : DI + CH].astype(jnp.bfloat16).reshape(seq_count, span_len, CH)
        )
        raw_steps = projected[:, DI + CH :].reshape(seq_count, span_len, HEADS)
        received = from_behind(conv_input[:, span_len - rim_width :], "group", 1)
        padded = jnp.concatenate([received, conv_input], axis=1).astype(jnp.float32)

        def prep_all(padded, raw_steps, kernel, shift_bias, step_shift, decay_rate):
            signal, inflow, write_map, read_map, log_decay = jax.vmap(
                prepare, in_axes=(0, 0, None, None, None, None, 0)
            )(padded, raw_steps, kernel, shift_bias, step_shift, decay_rate, tap_mask)
            return (signal, inflow, write_map, read_map, jnp.cumsum(log_decay, axis=1))

        prepared, prep_back = jax.vjp(
            prep_all, padded, raw_steps, kernel_real, shifts_real, steps_real, decays_real
        )
        signal, inflow, write_map, read_map, cum_decay = prepared

        def state_all(inflow, write_map, cum_decay):
            return jax.vmap(mix_state)(inflow, write_map, cum_decay, end_mask, total_mask)

        (through, local_state), state_back = jax.vjp(state_all, inflow, write_map, cum_decay)
        identity_pair = (jnp.ones_like(through), jnp.zeros_like(local_state))
        state_in = carried_in((through, local_state), "group", chain, identity_pair, False)[1]

        def out_all(signal, inflow, write_map, read_map, cum_decay, state_in, gate_z, skips, gains):
            return jax.vmap(mix_out, in_axes=(0, 0, 0, 0, 0, 0, 0, None, None, 0, 0))(
                signal,
                inflow,
                write_map,
                read_map,
                cum_decay,
                state_in,
                gate_z,
                skips,
                gains,
                same_doc,
                carry_mask,
            )

        gated_norm, out_back = jax.vjp(
            out_all,
            signal,
            inflow,
            write_map,
            read_map,
            cum_decay,
            state_in,
            gate_z,
            skips_real,
            gains_real,
        )
        gated_low = gated_norm.reshape(-1, DI).astype(jnp.bfloat16)
        branch = jnp.dot(gated_low, out_weight, preferred_element_type=jnp.float32)
        outputs.append((rows_in + branch).astype(jnp.bfloat16).reshape(tokens.shape[1:]))
        upstream = cotangent[batch_index].reshape(-1, D)
        grad_out_weight = contract_rows(gated_low, upstream)
        grad_mixed = contract_cols(upstream, out_weight).reshape(gated_norm.shape)
        (
            grad_signal,
            grad_inflow,
            grad_write,
            grad_read,
            grad_cum,
            grad_state,
            grad_gate,
            grad_skips,
            grad_gains,
        ) = out_back(grad_mixed)
        returned = carried_in((through, grad_state), "group", back_chain, identity_pair, True)[1]
        grad_through = jnp.sum(state_in * returned, axis=(2, 3))
        more_inflow, more_write, more_cum = state_back((grad_through, returned))
        grad_padded, grad_raw, grad_kernel, grad_shift, grad_stepb, grad_decay = prep_back(
            (
                grad_signal,
                grad_inflow + more_inflow,
                grad_write + more_write,
                grad_read,
                grad_cum + more_cum,
            )
        )
        rim_grads = from_behind(grad_padded[:, :rim_width], "group", -1)
        grad_conv = grad_padded[:, rim_width:] + jnp.concatenate(
            [jnp.zeros((seq_count, span_len - rim_width, CH), jnp.float32), rim_grads], axis=1
        )
        grad_projected = jnp.concatenate(
            [grad_gate.reshape(-1, DI), grad_conv.reshape(-1, CH), grad_raw.reshape(-1, HEADS)],
            axis=1,
        ).astype(jnp.bfloat16)
        grad_in_weight = contract_rows(normed_low, grad_projected)
        grad_normed = contract_cols(grad_projected, in_weight)
        grad_rows, grad_norm_gain = norm_back(grad_normed)
        input_grads.append(
            (upstream.astype(jnp.float32) + grad_rows)
            .astype(jnp.bfloat16)
            .reshape(tokens.shape[1:])
        )
        current = (
            grad_norm_gain,
            grad_in_weight,
            grad_kernel,
            grad_shift,
            grad_stepb,
            grad_decay,
            grad_skips,
            grad_gains,
            grad_out_weight,
        )
        totals = current if totals is None else jax.tree.map(jnp.add, totals, current)
    flat_len = master.shape[0] * lax.axis_size(DP)
    flat = jnp.concatenate(
        [piece.reshape(-1) for piece in totals] + [jnp.zeros((flat_len - NPARAM,), jnp.float32)]
    )
    quarter = sum_in_tiles(flat, DP_GROUP, 0)
    shard = collect(quarter, "group", 0)
    squares = over_copies(jnp.sum(shard * shard), DP)
    clip_factor = MAX_NORM / jnp.maximum(jnp.sqrt(squares), MAX_NORM)
    first_moment, second_moment, updated = adam_update(
        shard * clip_factor, master, moment_one, moment_two, step_count
    )
    copies = spread_gather(updated.astype(jnp.bfloat16), DP, 0)
    return (
        jnp.stack(outputs),
        jnp.stack(input_grads),
        shard,
        first_moment,
        second_moment,
        updated,
        copies,
    )


def solution(mesh):
    finer = Mesh(
        mesh.devices.reshape(4, 2, 4, mesh.shape["group"]), ("dp_0", "dp_1", "dp_2", "group")
    )
    return jax.shard_map(
        shards,
        mesh=finer,
        in_specs=(
            P(None, DP, "group", None),
            P(None, DP, None),
            P(None, DP, "group", None),
            P(),
            P(),
            P(),
            P(),
            P(),
            P(),
            P(),
            P(),
            P(),
            P(DP),
            P(DP),
            P(DP),
            P(),
        ),
        out_specs=(
            P(None, DP, "group", None),
            P(None, DP, "group", None),
            P(DP),
            P(DP),
            P(DP),
            P(DP),
            P(),
        ),
        check_vma=False,
    )
```

profile of v0, /device:TPU:1, one launch (start us, length us, event | category | flops | bytes accessed | tf_op | source)
XLA Modules:
  0.0 1562.1 jit_solution(13495260989748269464)
XLA Ops:
  59.8 13.2 collective-permute-start.1
  107.9 11.2 while.56
  123.8 10.1 bitcast_add_fusion.7
  164.6 11.2 while.57
  180.5 11.5 bitcast_add_fusion.6
  196.8 11.4 while.58
  237.2 14.7 fusion.25
  275.0 13.0 fusion.27
  321.2 12.1 multiply_reduce_fusion.7
  361.2 9.9 while.59
  474.3 14.9 convolution_add_fusion
  489.2 18.2 %copy.420 = f32[1024,4384]{1,0:T(8,128)} copy(f32[1024,4384]{0,1:T(8,128)} %convolution_add_fusion) | data formatting | bytes 35913728 | tf_op jit(solution)/shard_map/add | solution.py:385
  507.4 22.9 %reshape.1528 = f32[4489216]{0:T(1024)} reshape(f32[1024,4384]{1,0:T(8,128)} %copy.420) | data formatting | bytes 35913728 | tf_op jit(solution)/shard_map/reshape | solution.py:388
  530.4 210.1 %concatenate.72 = f32[6602752]{0:T(1024)} concatenate(f32[1024]{0:T(1024)S(1)} %add.426, f32[4489216]{0:T(1024)} %reshape.1528, f32[9216]{0:T(1024)S(1)} %copy-done.90, f32[2304]{0:T(1024)S(1)} %copy-done.103, f32[32]{0:T(128)S(1)} %copy-done.167, f32[32]{0:T(128)S(1)} %copy-done.165, f32[32]{0:T(128)S(1)} %copy-done.166, f32[2048]{0:T(1024)S(1)} %copy-done.105, ...), dimensions={0} | concatenate | bytes 52822016 | tf_op jit(solution)/shard_map/concatenate | solution.py:387
  740.5 25.4 %reshape.1535 = f32[128,51584]{1,0:T(8,128)} reshape(f32[6602752]{0:T(1024)} %concatenate.72) | data formatting | bytes 52822016 | tf_op jit(solution)/shard_map/reshape | solution.py:54
  765.9 17.7 %pad.112 = f32[128,52224]{1,0:T(8,128)} pad(f32[128,51584]{1,0:T(8,128)} %reshape.1535, f32[]{:T(128)} %constant.159.clone.1), padding=0_0x0_640 | pad | bytes 53149700 | tf_op jit(solution)/shard_map/jit(_pad)/pad | solution.py:63
  783.6 24.2 %reshape.1536 = f32[52224,128]{1,0:T(8,128)} reshape(f32[128,52224]{1,0:T(8,128)} %pad.112) | data formatting | bytes 53477376 | tf_op jit(solution)/shard_map/reshape | solution.py:63
  807.8 237.4 %all-reduce.46.cloned.1.call-done = f32[52224,128]{1,0:T(8,128)} async-done(((f32[52224,128]{1,0:T(8,128)}), f32[52224,128]{1,0:T(8,128)}) %all-reduce.46.cloned.1.call-update) | async-done | bytes 26738704
  1053.7 10.7 all-to-all-done
  1094.5 30.8 %all-reduce.40.cloned.1.call-done = bf16[275104]{0:T(1024)(128)(2,1)} async-done(((bf16[275104]{0:T(1024)(128)(2,1)}), bf16[275104]{0:T(1024)(128)(2,1)}) %all-reduce.40.cloned.1.call-update) | async-done | bytes 550224
  1127.7 44.5 %all-reduce.44.cloned.1.call-done = bf16[275136]{0:T(1024)(128)(2,1)} async-done(((bf16[275136]{0:T(1024)(128)(2,1)}), bf16[275136]{0:T(1024)(128)(2,1)}) %all-reduce.44.cloned.1.call-update) | async-done | bytes 550288
  1174.5 32.7 %all-reduce.42.cloned.1.call-done = bf16[137552]{0:T(1024)(128)(2,1)} async-done(((bf16[137552]{0:T(1024)(128)(2,1)}), bf16[137552]{0:T(1024)(128)(2,1)}) %all-reduce.42.cloned.1.call-update) | async-done | bytes 275120
  1209.4 26.0 %all-gather.35.cloned.1.call-done = bf16[2,4,68776]{2,1,0:T(4,128)(2,1)} async-done(((bf16[1,4,68776]{2,1,0:T(4,128)(2,1)}), bf16[2,4,68776]{2,1,0:T(4,128)(2,1)}) %all-gather.35.cloned.1.call-update) | async-done | bytes 1100432 | tf_op jit(solution)/shard_map/all_gather | solution.py:96
  1238.3 31.9 %all-gather.39.cloned.1.call-done = bf16[4,4,68784]{2,1,0:T(4,128)(2,1)} async-done(((bf16[1,4,68784]{2,1,0:T(4,128)(2,1)}), bf16[4,4,68784]{2,1,0:T(4,128)(2,1)}) %all-gather.39.cloned.1.call-update) | async-done | bytes 2201104 | tf_op jit(solution)/shard_map/all_gather | solution.py:96
  1273.5 21.8 %all-gather.37.cloned.1.call-done = bf16[4,2,68776]{2,1,0:T(2,128)(2,1)} async-done(((bf16[1,2,68776]{2,1,0:T(2,128)(2,1)}), bf16[4,2,68776]{2,1,0:T(2,128)(2,1)}) %all-gather.37.cloned.1.call-update) | async-done | bytes 1100432 | tf_op jit(solution)/shard_map/all_gather | solution.py:96
  1307.6 40.7 %all-gather.21.cloned.1.call-done = bf16[32,68776]{1,0:T(8,128)(2,1)} async-done(((bf16[8,68776]{1,0:T(8,128)(2,1)}), bf16[32,68776]{1,0:T(8,128)(2,1)}) %all-gather.21.cloned.1.call-update) | async-done | bytes 4401680 | tf_op jit(solution)/shard_map/all_gather | solution.py:96
  1348.3 22.9 %dynamic-update-slice.3 = bf16[32,206336]{1,0:T(8,128)(2,1)} dynamic-update-slice(bf16[32,206336]{1,0:T(8,128)(2,1)} %custom-call.4, bf16[32,68776]{1,0:T(8,128)(2,1)} %all-gather.21.cloned.1.call-done, s32[]{} %constant.275, s32[]{} %constant.275) | dynamic-update-slice | bytes 8803332
  1371.2 41.5 %all-gather.25.cloned.1.call-done = bf16[32,68784]{1,0:T(8,128)(2,1)} async-done(((bf16[16,68784]{1,0:T(8,128)(2,1)}), bf16[32,68784]{1,0:T(8,128)(2,1)}) %all-gather.25.cloned.1.call-update) | async-done | bytes 4402192 | tf_op jit(solution)/shard_map/all_gather | solution.py:96
  1429.9 35.3 %all-gather.23.cloned.1.call-done = bf16[32,68776]{1,0:T(8,128)(2,1)} async-done(((bf16[8,68776]{1,0:T(8,128)(2,1)}), bf16[32,68776]{1,0:T(8,128)(2,1)}) %all-gather.23.cloned.1.call-update) | async-done | bytes 4401680 | tf_op jit(solution)/shard_map/all_gather | solution.py:96
  1482.5 24.9 %dynamic-update-slice.4 = bf16[32,206336]{1,0:T(8,128)(2,1)} dynamic-update-slice(bf16[32,206336]{1,0:T(8,128)(2,1)} %dynamic-update-slice.3, bf16[32,68776]{1,0:T(8,128)(2,1)} %reshape.1539, s32[]{} %constant.275, s32[]{} %constant.276) | dynamic-update-slice | bytes 8803332
  1507.4 24.7 %dynamic-update-slice.5 = bf16[32,206336]{1,0:T(8,128)(2,1)} dynamic-update-slice(bf16[32,206336]{1,0:T(8,128)(2,1)} %dynamic-update-slice.4, bf16[32,68784]{1,0:T(8,128)(2,1)} %reshape.1541, s32[]{} %constant.275, s32[]{} %constant.277) | dynamic-update-slice | bytes 8804356 | tf_op jit(solution)/shard_map/concatenate | solution.py:112
  1532.0 23.3 %reshape.1542 = bf16[6602752]{0:T(1024)(128)(2,1)} reshape(bf16[32,206336]{1,0:T(8,128)(2,1)} %dynamic-update-slice.5) | data formatting | bytes 26411008 | tf_op jit(solution)/shard_map/reshape | solution.py:71
  (666 shorter events, 482.1 us)
Async XLA Ops:
  7.2 100.7 %all-gather.27.cloned.1.call-start = ((), (), s32[]{:S(2)}) async-start(), calls=%async_computation.5 | async-start | bytes 5242880 | tf_op jit(solution)/shard_map/all_gather | solution.py:37
  19.2 25.9 %collective-permute-start = (bf16[1,3,2304]{2,1,0:T(4,128)(2,1)S(1)}, bf16[1,3,2304]{2,1,0:T(4,128)(2,1)S(1)}, u32[]{:S(2)}, u32[]{:S(2)}) collective-permute-start(bf16[1,3,2304]{2,1,0:T(4,128)(2,1)S(1)} %copy.371), channel_id=1, source_target_pairs={{0,1},{1,2},{2,3},{4,5},{5,6},{6,7},{8,9},{9,10},{10,11},{12,13},{... | collective-permute-start | bytes 41480 | tf_op jit(solution)/shard_map/ppermute | solution.py:32
  39.8 35.5 %copy-start.140 = (f32[1,256]{1,0:T(1,128)}, f32[1,256]{1,0:T(1,128)S(1)}, u32[]{:S(2)}) copy-start(f32[1,256]{1,0:T(1,128)S(1)} %get-tuple-element.667) | copy-start | bytes 3076
  42.7 34.0 %copy-start.114 = (f32[1,256]{1,0:T(1,128)}, f32[1,256]{1,0:T(1,128)S(1)}, u32[]{:S(2)}) copy-start(f32[1,256]{1,0:T(1,128)S(1)} %get-tuple-element.730) | copy-start | bytes 3076
  45.1 36.4 %copy-start.79 = (f32[2304]{0:T(1024)}, f32[2304]{0:T(1024)S(1)}, u32[]{:S(2)}) copy-start(f32[2304]{0:T(1024)S(1)} %get-tuple-element.595) | copy-start | bytes 27652
  56.5 108.1 %all-gather.29.cloned.1.call-start = ((), (), s32[]{:S(2)}) async-start(), calls=%async_computation.6 | async-start | bytes 5242880 | tf_op jit(solution)/shard_map/all_gather | solution.py:37
  59.8 18.3 %collective-permute-start.1 = (bf16[1,3,2304]{2,1,0:T(4,128)(2,1)S(1)}, bf16[1,3,2304]{2,1,0:T(4,128)(2,1)S(1)}, u32[]{:S(2)}, u32[]{:S(2)}) collective-permute-start(bf16[1,3,2304]{2,1,0:T(4,128)(2,1)S(1)} %copy.383), channel_id=1, source_target_pairs={{0,1},{1,2},{2,3},{4,5},{5,6},{6,7},{8,9},{9,10},{10,11},{12,13},{... | collective-permute-start | bytes 41480 | tf_op jit(solution)/shard_map/ppermute | solution.py:32
  91.4 100.7 %all-gather.31.cloned.1.call-start = ((), (), s32[]{:S(2)}) async-start(), calls=%async_computation.7 | async-start | bytes 5242880 | tf_op jit(solution)/shard_map/all_gather | solution.py:37
  96.8 241.6 %copy-start.66 = (f32[2048]{0:T(1024)}, f32[2048]{0:T(1024)S(1)}, u32[]{:S(2)}) copy-start(f32[2048]{0:T(1024)S(1)} %convert_element_type.168) | copy-start | bytes 24580
  148.2 208.2 %all-gather.33.cloned.1.call-start = ((), (), s32[]{:S(2)}) async-start(), calls=%async_computation.8 | async-start | bytes 5242880 | tf_op jit(solution)/shard_map/all_gather | solution.py:37
  237.1 808.1 %all-reduce.46.cloned.1.call-start = ((), (), s32[]{:S(2)}) async-start(), calls=%async_computation.15 | async-start | bytes 53477376
  426.8 17.3 %collective-permute-start.3 = (f32[1,3,2304]{2,0,1:T(1,128)}, f32[1,3,2304]{2,0,1:T(1,128)}, u32[]{:S(2)}, u32[]{:S(2)}) collective-permute-start(f32[1,3,2304]{2,0,1:T(1,128)} %copy.412), channel_id=1, source_target_pairs={{1,0},{2,1},{3,2},{5,4},{6,5},{7,6},{9,8},{10,9},{11,10},{13,12},{... | collective-permute-start | bytes 82952 | tf_op jit(solution)/shard_map/ppermute | solution.py:32
  431.3 19.2 %collective-permute-start.2 = (f32[1,3,2304]{2,0,1:T(1,128)}, f32[1,3,2304]{2,0,1:T(1,128)}, u32[]{:S(2)}, u32[]{:S(2)}) collective-permute-start(f32[1,3,2304]{2,0,1:T(1,128)} %copy.397), channel_id=1, source_target_pairs={{1,0},{2,1},{3,2},{5,4},{6,5},{7,6},{9,8},{10,9},{11,10},{13,12},{... | collective-permute-start | bytes 82952 | tf_op jit(solution)/shard_map/ppermute | solution.py:32
  507.4 23.0 %copy-start.105 = (f32[2048]{0:T(1024)S(1)}, f32[2048]{0:T(1024)}, u32[]{:S(2)}) copy-start(f32[2048]{0:T(1024)} %add.433) | copy-start | bytes 24580
  507.4 23.0 %copy-start.165 = (f32[32]{0:T(128)S(1)}, f32[32]{0:T(128)}, u32[]{:S(2)}) copy-start(f32[32]{0:T(128)} %add_multiply_fusion) | copy-start | bytes 388
  507.4 23.0 %copy-start.166 = (f32[32]{0:T(128)S(1)}, f32[32]{0:T(128)}, u32[]{:S(2)}) copy-start(f32[32]{0:T(128)} %add.432) | copy-start | bytes 388
  507.4 23.0 %copy-start.167 = (f32[32]{0:T(128)S(1)}, f32[32]{0:T(128)}, u32[]{:S(2)}) copy-start(f32[32]{0:T(128)} %add.430) | copy-start | bytes 388
  807.8 244.6 %copy-start.178 = (u32[128]{0:T(128)S(1)}, u32[128]{0:T(128)}, u32[]{:S(2)}) copy-start(u32[128]{0:T(128)} %constant.243) | copy-start | bytes 1540
  1047.5 16.9 %all-to-all-start = ((f32[4,1,51584]{2,1,0:T(1,128)}), f32[4,1,51584]{2,1,0:T(1,128)S(1)}, u32[]{:S(2)}, u32[]{:S(2)}) async-start(f32[4,1,51584]{2,1,0:T(1,128)} %broadcast_in_dim.205), calls=%async_computation | async-start | bytes 1650688 | tf_op jit(solution)/shard_map/all_to_all | solution.py:76
  1066.7 12.7 all-to-all-start.1
  1072.3 53.1 %all-reduce.40.cloned.1.call-start = ((), (), s32[]{:S(2)}) async-start(), calls=%async_computation.9 | async-start | bytes 1101824
  1087.2 85.0 %all-reduce.44.cloned.1.call-start = ((), (), s32[]{:S(2)}) async-start(), calls=%async_computation.11 | async-start | bytes 1101824
  1091.0 116.3 %all-reduce.42.cloned.1.call-start = ((), (), s32[]{:S(2)}) async-start(), calls=%async_computation.10 | async-start | bytes 552960
  1094.5 140.9 %all-gather.35.cloned.1.call-start = ((), (), s32[]{:S(2)}) async-start(), calls=%async_computation.12 | async-start | bytes 1652736 | tf_op jit(solution)/shard_map/all_gather | solution.py:96
  1127.7 142.5 %all-gather.39.cloned.1.call-start = ((), (), s32[]{:S(2)}) async-start(), calls=%async_computation.14 | async-start | bytes 2754560 | tf_op jit(solution)/shard_map/all_gather | solution.py:96
  1174.5 120.9 %all-gather.37.cloned.1.call-start = ((), (), s32[]{:S(2)}) async-start(), calls=%async_computation.13 | async-start | bytes 1377280 | tf_op jit(solution)/shard_map/all_gather | solution.py:96
  1209.3 139.0 %all-gather.21.cloned.1.call-start = ((), (), s32[]{:S(2)}) async-start(), calls=%async_computation.2 | async-start | bytes 5509120 | tf_op jit(solution)/shard_map/all_gather | solution.py:96
  1238.2 174.5 %all-gather.25.cloned.1.call-start = ((), (), s32[]{:S(2)}) async-start(), calls=%async_computation.4 | async-start | bytes 6610944 | tf_op jit(solution)/shard_map/all_gather | solution.py:96
  1273.4 25.0 %copy-start.23 = (f32[1,256,2048]{1,2,0:T(8,128)S(1)}, f32[1,256,2048]{1,2,0:T(8,128)}, u32[]{:S(2)}) copy-start(f32[1,256,2048]{1,2,0:T(8,128)} %copy-done.21) | copy-start | bytes 6291460
  1273.4 25.0 %copy-start.67 = (f32[2048]{0:T(1024)S(1)}, f32[2048]{0:T(1024)}, u32[]{:S(2)}) copy-start(f32[2048]{0:T(1024)} %copy-done.66) | copy-start | bytes 24580
  1273.4 25.0 %copy-start.113 = (f32[256]{0:T(256)S(1)}, f32[256]{0:T(256)}, u32[]{:S(2)}) copy-start(f32[256]{0:T(256)} %copy-done.111) | copy-start | bytes 3076
  1273.5 191.7 %all-gather.23.cloned.1.call-start = ((), (), s32[]{:S(2)}) async-start(), calls=%async_computation.3 | async-start | bytes 5509120 | tf_op jit(solution)/shard_map/all_gather | solution.py:96
  (174 other events, 897.0 us)
Sparse Core Ops, SparseCore 0:
  56.6 37.9 all-gather.26
  96.3 37.8 all-gather.28
  148.4 38.2 all-gather.30
  237.3 38.3 all-gather.32
  807.9 237.2 all-reduce.45
  1087.3 38.0 all-reduce.39
  1128.3 43.8 all-reduce.43
  1174.8 32.4 all-reduce.41
  1209.5 25.8 all-gather.34
  1237.5 32.6 all-gather.38
  1271.9 23.4 all-gather.36
  1296.9 51.4 all-gather.20
  1350.6 62.0 all-gather.24
  1414.2 50.9 all-gather.22
where the time goes:
time: 1590 us; the launch traced here: 1560 us
  local copies, waits for them, and re-layouts  589 us (37%)
  waiting for transfers between devices  558 us (35%)
  matrix products  183 us (12%)
  other arithmetic  160 us (10%)
  starting transfers between devices  34.7 us (2%)
  between operations  22.4 us (1%)
    unnamed x18, waiting for transfers between devices  346 us
    concatenate x1, local copies, waits for them, and re-layouts, shards(): jnp.concatenate([piece.reshape(-1) for piece in totals] + [jnp.zeros((fla...  210 us
    all_gather x6, waiting for transfers between devices, gather_in_order(): parts = lax.all_gather(parts, axes[k], axis=0, tiled=True)  197 us
    unnamed x390, local copies, waits for them, and re-layouts  100 us
    dot_general x6, matrix products, mix_out(): jnp.einsum('ijh,ij,jhp->ihp', kernel, intersection, inflow, precision=HIG...  64.9 us
    dot_general x4, matrix products, contract_rows(): lax.dot_general(left, right, (((0,), (0,)), ((), ())), preferred_element_...  33.9 us
  transfers between devices with their start and end apart: 20, of which 12 were waited for; matrix products, arithmetic and copies ran while one was open for 21% of the time, Pallas kernels for 0%

commit v1 on v0

--- a/solution.py
+++ b/solution.py
@@ -1,6 +1,8 @@
 import jax
 import jax.numpy as jnp
 from jax import lax
+from jax.experimental import pallas as pl
+from jax.experimental.pallas import tpu as pltpu
 from jax.sharding import Mesh
 from jax.sharding import PartitionSpec as P
 
@@ -12,8 +14,8 @@
 KCONV = 4
 CH = 2304
 NPARAM = 6601056
-DP = ("dp_0", "dp_1", "dp_2")
-DP_GROUP = ("dp_0", "dp_1", "dp_2", "group")
+DP = ("y", "zl", "x")
+GROUP = ("zh", "core")
 
 
 EPSILON = 1e-05
@@ -49,67 +51,331 @@
     return lax.fori_loop(0, count - 1, step, running)
 
 
-def split_up(shard, dim, size):
-    lengths = shard.shape
-    parts = shard.reshape(*lengths[:dim], size, lengths[dim] // size, *lengths[dim + 1 :])
-    return jnp.moveaxis(parts, dim, 0)
-
-
-def sum_in_tiles(shard, axis, dim):
-    size = lax.axis_size(axis)
-    parts = split_up(shard, dim, size)
-    lines = parts.reshape(size, -1)
-    extent = max(16, -(-lines.shape[1] // 1024) * 8)
-    lines = jnp.pad(lines, ((0, 0), (0, extent * 128 - lines.shape[1]))).reshape(-1, 128)
-    own = lax.psum_scatter(lines, axis, scatter_dimension=0, tiled=True)
-    return own.reshape(-1)[: parts[0].size].reshape(parts.shape[1:])
-
-
-def laid_out(parts, dim):
-    parts = jnp.moveaxis(parts, 0, dim)
-    lengths = parts.shape
-    return parts.reshape(*lengths[:dim], lengths[dim] * lengths[dim + 1], *lengths[dim + 2 :])
-
-
 def sent_to_all(shard, axis):
     copies = jnp.broadcast_to(shard, (lax.axis_size(axis), *shard.shape))
     return lax.all_to_all(copies, axis, split_axis=0, concat_axis=0, tiled=True)
 
 
-def collect(shard, axis, dim):
-    return laid_out(sent_to_all(shard, axis), dim)
-
-
 def over_copies(shard, axis):
     everything = sent_to_all(shard, axis)
     return jnp.sum(everything, axis=0)
 
 
-def edges_of(length, count):
-    unit = 8 if length >= 8 * count else 1
-    return [length // unit * k // count * unit for k in range(1, count)]
-
-
-def gather_in_order(shard, axes, sequence):
-    parts = shard[None]
-    for k in sequence:
-        parts = lax.all_gather(parts, axes[k], axis=0, tiled=True)
-    block = [lax.axis_size(axes[k]) for k in reversed(sequence)]
-    parts = parts.reshape(*block, *shard.shape)
-    turned = sorted(range(len(sequence)), key=lambda place: sequence[len(sequence) - 1 - place])
-    return parts.transpose(*turned, *range(len(sequence), parts.ndim)).reshape(-1, *shard.shape)
-
-
-def spread_gather(shard, axes, dim):
-    numbers = list(range(len(axes)))[::-1]
-    widest = shard.shape.index(max(shard.shape[:-1] or shard.shape))
-    edges = [0, *edges_of(shard.shape[widest], len(axes)), shard.shape[widest]]
-    outs = []
-    for k, (start, end) in enumerate(zip(edges, edges[1:])):
-        if end > start:
-            slab = lax.slice_in_dim(shard, start, end, axis=widest)
-            outs.append(gather_in_order(slab, axes, numbers[k:] + numbers[:k]))
-    return laid_out(jnp.concatenate(outs, axis=widest + 1), dim)
+LANES = 128
+LINES = 51584
+SHARD_LINES = 1612
+IN_LINE = 8
+MID_LINE = 35080
+OUT_LINE = 35187
+PIECE = 416
+PARTS = ((0, 144), (144, 144), (288, 128))
+TAIL_LINES = 51632
+GROUP_LINES = 137
+RING = {"x": ("x",), "y": ("y",), "z": ("zl", "zh")}
+ROUTES = (("x", "z", "y"), ("y", "z", "x"), ("z", "x", "y"))
+
+
+def ring_place(axis, i):
+    i = i % 4
+    return (i % 2) * 2 + i // 2 if axis == "z" else i
+
+
+def from_offset(block, axis, distance):
+    route = [(ring_place(axis, i + distance), ring_place(axis, i)) for i in range(4)]
+    return lax.ppermute(block, RING[axis], route)
+
+
+def swap_cores(block):
+    return lax.ppermute(block, "core", [(0, 1), (1, 0)])
+
+
+def position():
+    z = 2 * lax.axis_index("zh") + lax.axis_index("zl")
+    return jnp.stack([lax.axis_index("y"), z, lax.axis_index("x"), lax.axis_index("core")]).astype(jnp.int32)
+
+
+def first_tile(shard):
+    return (403 * shard) // 4
+
+
+def pack_kernel(pos, left, right, gated, cot, gain_part, mid_part, *rest):
+    keep, send = rest[:3], rest[3:6]
+    flat, carry, edge, stage, sems = rest[6:]
+    lane = lax.broadcasted_iota(jnp.int32, (256, LANES), 1)
+
+    flat[0:IN_LINE, :] = gain_part[...]
+    flat[MID_LINE : MID_LINE + 104, :] = mid_part[0:104, :]
+    flat[MID_LINE + 104 : MID_LINE + 107, :] = mid_part[104:107, :]
+    carry[...] = jnp.zeros_like(carry)
+    for k in range(4):
+
+        def put(tile, line, k=k):
+            moved = pltpu.roll(tile, 32 * k, 1) if k else tile
+            whole = jnp.where(lane < 32 * k, carry[...], moved) if k else moved
+            flat[pl.ds(line, 256, stride=GROUP_LINES), :] = whole
+            carry[...] = moved
+            return whole
+
+        def columns(j, _, k=k, put=put):
+            block = right[:, pl.ds(pl.multiple_of(j * 512, 512), 512)]
+            product = jnp.dot(left[k], block, preferred_element_type=jnp.float32)
+            for t in range(4):
+                put(product[:, t * LANES : (t + 1) * LANES], IN_LINE + 34 * k + 4 * j + t)
+            return 0
+
+        lax.fori_loop(0, 8, columns, 0)
+        product = jnp.dot(left[k], right[:, 4096:4480], preferred_element_type=jnp.float32)
+        for t in range(3):
+            whole = put(product[:, t * LANES : (t + 1) * LANES], IN_LINE + 34 * k + 32 + t)
+        carry[...] = whole
+
+    edge[0:8, :] = mid_part[99:107, :]
+
+    def rows(b, _):
+        block = gated[pl.ds(pl.multiple_of(b * 256, 256), 256), :]
+        product = jnp.dot(block, cot[...], preferred_element_type=jnp.float32)
+        start = OUT_LINE + 2048 * b
+        for t in range(7):
+            flat[pl.ds(start + t, 256, stride=8), :] = product[:, t * LANES : (t + 1) * LANES]
+        last = product[:, 7 * LANES :]
+        edge[8:264, :] = last
+        flat[pl.ds(start - 1, 256, stride=8), :] = jnp.where(lane < 96, edge[7:263, :], last)
+        edge[0:8, :] = edge[256:264, :]
+        return 0
+
+    lax.fori_loop(0, 8, rows, 0)
+    low = lax.broadcasted_iota(jnp.int32, (1, LANES), 1) < 96
+    flat[OUT_LINE + 16383 : TAIL_LINES, :] = jnp.zeros((TAIL_LINES - OUT_LINE - 16383, LANES), jnp.float32)
+    flat[OUT_LINE + 16383 : OUT_LINE + 16384, :] = jnp.where(low, edge[7:8, :], 0.0)
+
+    my_y, my_z, my_x, my_core = pos[0], pos[1], pos[2], pos[3]
+
+    def drain(slot):
+        pltpu.make_async_copy(stage.at[slot], keep[0].at[pl.ds(0, PIECE)], sems.at[slot]).wait()
+
+    def ship(i, _):
+        slot = i % 2
+
+        @pl.when(i >= 2)
+        def _():
+            drain(slot)
+
+        shard, quarter = i // 4, i % 4
+        line = 16 * first_tile(shard) + PIECE * quarter
+        stage[slot] = flat[pl.ds(pl.multiple_of(line, 16), PIECE), :].astype(jnp.bfloat16)
+        x, zl, y = shard % 4, (shard // 4) % 2, shard // 8
+        z, core = 2 * (quarter // 2) + zl, quarter % 2
+        off = {"y": (y - my_y + 4) % 4, "z": (z - my_z + 4) % 4, "x": (x - my_x + 4) % 4}
+        for p, (start, size) in enumerate(PARTS):
+            a, b, c = (off[axis] for axis in ROUTES[p])
+            to = pl.ds(pl.multiple_of(((a * 4 + b) * 4 + c) * size, 16), size)
+            source = stage.at[slot, pl.ds(start, size)]
+
+            @pl.when(core == my_core)
+            def _():
+                pltpu.make_async_copy(source, keep[p].at[to], sems.at[slot]).start()
+
+            @pl.when(core != my_core)
+            def _():
+                pltpu.make_async_copy(source, send[p].at[to], sems.at[slot]).start()
+
+        return 0
+
+    lax.fori_loop(0, 128, ship, 0)
+    drain(0)
+    drain(1)
+
+
+def pack(pos, left, right, gated, cot, gain_part, mid_part):
+    vmem, hbm = pl.BlockSpec(memory_space=pltpu.VMEM), pl.BlockSpec(memory_space=pl.ANY)
+    shapes = [jax.ShapeDtypeStruct((64 * size, LANES), jnp.bfloat16) for _, size in PARTS]
+    return pl.pallas_call(
+        pack_kernel,
+        out_shape=shapes + shapes,
+        in_specs=[pl.BlockSpec(memory_space=pltpu.SMEM)] + [vmem] * 6,
+        out_specs=[hbm] * 6,
+        scratch_shapes=[
+            pltpu.VMEM((TAIL_LINES, LANES), jnp.float32),
+            pltpu.VMEM((256, LANES), jnp.float32),
+            pltpu.VMEM((264, LANES), jnp.float32),
+            pltpu.VMEM((2, PIECE, LANES), jnp.bfloat16),
+            pltpu.SemaphoreType.DMA((2,)),
+        ],
+        compiler_params=pltpu.CompilerParams(vmem_limit_bytes=60 * 2**20),
+        cost_estimate=pl.CostEstimate(flops=7_000_000_000, bytes_accessed=25_000_000, transcendentals=0),
+        name="pack_gradients",
+    )(pos, left, right, gated, cot, gain_part, mid_part)
+
+
+def real(v):
+    return v.astype(jnp.float32)
+
+
+def low(v):
+    return v.astype(jnp.bfloat16)
+
+
+def reduce_pieces(keep, send):
+    got = [swap_cores(block) for block in send]
+    held = [low(real(mine) + real(other)) for mine, other in zip(keep, got)]
+
+    def hop(block, axis, narrow):
+        quarter = block.shape[0] // 4
+        total = real(block[:quarter])
+        moved = [to_offset(block[d * quarter : (d + 1) * quarter], axis, d) for d in range(1, 4)]
+        for part in moved:
+            total = total + real(part)
+        return low(total) if narrow else total
+
+    held = [hop(block, ROUTES[p][0], True) for p, block in enumerate(held)]
+    n0, n1 = PARTS[0][1] * 4, PARTS[1][1] * 4
+    both = jnp.concatenate(
+        [part for d in range(4) for part in (held[0][d * n0 : (d + 1) * n0], held[1][d * n1 : (d + 1) * n1])]
+    )
+    both, third = hop(both, "z", True), hop(held[2], "x", True)
+    n0, n2 = PARTS[0][1], PARTS[2][1]
+    first, second = both[: 4 * n0], both[4 * n0 :]
+    outer = jnp.concatenate(
+        [part for d in range(4) for part in (first[d * n0 : (d + 1) * n0], third[d * n2 : (d + 1) * n2])]
+    )
+    outer, second = hop(outer, "y", False), hop(second, "x", False)
+    return jnp.concatenate([outer[:n0], second, outer[n0:]])
+
+
+def to_offset(block, axis, distance):
+    route = [(ring_place(axis, i), ring_place(axis, i + distance)) for i in range(4)]
+    return lax.ppermute(block, RING[axis], route)
+
+
+def gather_pieces(piece):
+    def spread(block, axis):
+        return [block] + [from_offset(block, axis, d) for d in range(1, 4)]
+
+    n0, n1, n2 = (size for _, size in PARTS)
+    first, second, third = piece[:n0], piece[n0 : n0 + n1], piece[n0 + n1 :]
+    outer = spread(jnp.concatenate([first, third]), "y")
+    second = jnp.concatenate(spread(second, "x"))
+    first = jnp.concatenate([block[:n0] for block in outer])
+    third = jnp.concatenate([block[n0:] for block in outer])
+    both = spread(jnp.concatenate([first, second]), "z")
+    third = jnp.concatenate(spread(third, "x"))
+    first = jnp.concatenate([block[: 4 * n0] for block in both])
+    second = jnp.concatenate([block[4 * n0 :] for block in both])
+    mine = spread(first, "x") + spread(second, "y") + spread(third, "z")
+    return mine + [swap_cores(block) for block in mine]
+
+
+def unpack_kernel(pos, *rest):
+    sources, out = rest[:24], rest[24]
+    tiles, sem = rest[25:]
+    my_y, my_z, my_x, my_core = pos[0], pos[1], pos[2], pos[3]
+
+    def place(p, static, outer, inner, core):
+        off = dict(zip(ROUTES[p], (static, outer, inner)))
+        y, z, x = (my_y + off["y"]) % 4, (my_z + off["z"]) % 4, (my_x + off["x"]) % 4
+        shard = (y * 2 + z % 2) * 4 + x
+        return shard, 2 * (z // 2) + core
+
+    for p, (start, size) in enumerate(PARTS):
+        for far in range(4):
+            for other in range(2):
+                source = sources[other * 12 + p * 4 + far]
+
+                def move(i, _, p=p, far=far, other=other, source=source, start=start, size=size):
+                    core = (my_core + other) % 2
+                    shard, quarter = place(p, far, i // 4, i % 4, core)
+                    line = pl.multiple_of(16 * first_tile(shard) + PIECE * quarter + start, 16)
+                    here = pl.multiple_of(i * size, 16)
+                    if p == 0:
+
+                        @pl.when(quarter == 0)
+                        def _():
+                            pltpu.make_async_copy(
+                                source.at[pl.ds(pl.multiple_of(here + 16, 16), size - 16)],
+                                out.at[pl.ds(pl.multiple_of(line + 16, 16), size - 16)], sem
+                            ).start()
+
+                        @pl.when(quarter != 0)
+                        def _():
+                            pltpu.make_async_copy(source.at[pl.ds(here, size)], out.at[pl.ds(line, size)], sem).start()
+
+                    elif p == 1:
+                        pltpu.make_async_copy(source.at[pl.ds(here, size)], out.at[pl.ds(line, size)], sem).start()
+                    else:
+
+                        @pl.when(quarter == 3)
+                        def _():
+                            pltpu.make_async_copy(source.at[pl.ds(here, 80)], out.at[pl.ds(line, 80)], sem).start()
+
+                        @pl.when(quarter != 3)
+                        def _():
+                            pltpu.make_async_copy(source.at[pl.ds(here, size)], out.at[pl.ds(line, size)], sem).start()
+
+                    return 0
+
+                lax.fori_loop(0, 16, move, 0)
+    for far in range(4):
+        for other in range(2):
+
+            @pl.when((my_core + other) % 2 == 0)
+            def _(far=far, other=other):
+                def head(i, _):
+                    shard, quarter = place(0, far, i // 4, i % 4, 0)
+
+                    @pl.when(quarter == 0)
+                    def _():
+                        pltpu.make_async_copy(
+                            sources[other * 12 + far].at[pl.ds(pl.multiple_of(i * 144, 16), 16)], tiles.at[0, shard], sem
+                        ).start()
+
+                    return 0
+
+                lax.fori_loop(0, 16, head, 0)
+
+            @pl.when((my_core + other) % 2 == 1)
+            def _(far=far, other=other):
+                def tail(i, _):
+                    shard, quarter = place(2, far, i // 4, i % 4, 1)
+
+                    @pl.when(quarter == 3)
+                    def _():
+                        x = shard % 4
+                        skip = jnp.where((x == 1) | (x == 2), 80, 64)
+                        pltpu.make_async_copy(
+                            sources[other * 12 + 8 + far].at[pl.ds(pl.multiple_of(i * 128 + skip, 16), 16)],
+                            tiles.at[1, shard],
+                            sem,
+                        ).start()
+
+                    return 0
+
+                lax.fori_loop(0, 16, tail, 0)
+    moved = 128 * PIECE - 32 * 16 - 32 * 48
+    pltpu.make_async_copy(out.at[pl.ds(0, moved)], out.at[pl.ds(0, moved)], sem).wait()
+    pltpu.make_async_copy(tiles, tiles, sem).wait()
+    row = lax.broadcasted_iota(jnp.int32, (16, LANES), 0)
+    for shard in range(32):
+        x = shard % 4
+        if x:
+            joined = jnp.where(row < (12 * x) % 16, real(tiles[1, shard - 1]), real(tiles[0, shard]))
+            tiles[0, shard] = low(joined)
+    for shard in range(32):
+        pltpu.make_async_copy(tiles.at[0, shard], out.at[pl.ds(16 * ((403 * shard) // 4), 16)], sem).start()
+    pltpu.make_async_copy(tiles.at[0], tiles.at[0], sem).wait()
+
+
+def unpack(pos, pieces):
+    hbm, vmem = pl.BlockSpec(memory_space=pl.ANY), pl.BlockSpec(memory_space=pltpu.VMEM)
+    return pl.pallas_call(
+        unpack_kernel,
+        out_shape=jax.ShapeDtypeStruct((LINES, LANES), jnp.bfloat16),
+        in_specs=[pl.BlockSpec(memory_space=pltpu.SMEM)] + [vmem] * 24,
+        out_specs=hbm,
+        scratch_shapes=[pltpu.VMEM((2, 32, 16, LANES), jnp.bfloat16), pltpu.SemaphoreType.DMA],
+        compiler_params=pltpu.CompilerParams(vmem_limit_bytes=32 * 2**20),
+        cost_estimate=pl.CostEstimate(flops=0, bytes_accessed=27_000_000, transcendentals=0),
+        name="unpack_weights",
+    )(pos, *pieces)
 
 
 def norm_piece(values, scaling):
@@ -250,11 +516,12 @@
     decays_real = decay_log.astype(jnp.float32)
     skips_real = skip_gain.astype(jnp.float32)
     gains_real = gate_gain.astype(jnp.float32)
-    group_place = lax.axis_index("group")
+    group_place = lax.axis_index(GROUP)
     filler = jnp.full((seq_count, rim_width), -1, jnp.int32)
     outputs = []
     input_grads = []
     totals = None
+    factors = []
     for batch_index in range(micro_count):
         seg_window = lax.dynamic_slice_in_dim(
             jnp.concatenate([filler, segments[batch_index]], axis=1),
@@ -278,7 +545,7 @@
             projected[:, DI : DI + CH].astype(jnp.bfloat16).reshape(seq_count, span_len, CH)
         )
         raw_steps = projected[:, DI + CH :].reshape(seq_count, span_len, HEADS)
-        received = from_behind(conv_input[:, span_len - rim_width :], "group", 1)
+        received = from_behind(conv_input[:, span_len - rim_width :], GROUP, 1)
         padded = jnp.concatenate([received, conv_input], axis=1).astype(jnp.float32)
 
         def prep_all(padded, raw_steps, kernel, shift_bias, step_shift, decay_rate):
@@ -297,7 +564,7 @@
 
         (through, local_state), state_back = jax.vjp(state_all, inflow, write_map, cum_decay)
         identity_pair = (jnp.ones_like(through), jnp.zeros_like(local_state))
-        state_in = carried_in((through, local_state), "group", chain, identity_pair, False)[1]
+        state_in = carried_in((through, local_state), GROUP, chain, identity_pair, False)[1]
 
         def out_all(signal, inflow, write_map, read_map, cum_decay, state_in, gate_z, skips, gains):
             return jax.vmap(mix_out, in_axes=(0, 0, 0, 0, 0, 0, 0, None, None, 0, 0))(
@@ -330,7 +597,6 @@
         branch = jnp.dot(gated_low, out_weight, preferred_element_type=jnp.float32)
         outputs.append((rows_in + branch).astype(jnp.bfloat16).reshape(tokens.shape[1:]))
         upstream = cotangent[batch_index].reshape(-1, D)
-        grad_out_weight = contract_rows(gated_low, upstream)
         grad_mixed = contract_cols(upstream, out_weight).reshape(gated_norm.shape)
         (
             grad_signal,
@@ -343,7 +609,7 @@
             grad_skips,
             grad_gains,
         ) = out_back(grad_mixed)
-        returned = carried_in((through, grad_state), "group", back_chain, identity_pair, True)[1]
+        returned = carried_in((through, grad_state), GROUP, back_chain, identity_pair, True)[1]
         grad_through = jnp.sum(state_in * returned, axis=(2, 3))
         more_inflow, more_write, more_cum = state_back((grad_through, returned))
         grad_padded, grad_raw, grad_kernel, grad_shift, grad_stepb, grad_decay = prep_back(
@@ -355,7 +621,7 @@
                 grad_cum + more_cum,
             )
         )
-        rim_grads = from_behind(grad_padded[:, :rim_width], "group", -1)
+        rim_grads = from_behind(grad_padded[:, :rim_width], GROUP, -1)
         grad_conv = grad_padded[:, rim_width:] + jnp.concatenate(
             [jnp.zeros((seq_count, span_len - rim_width, CH), jnp.float32), rim_grads], axis=1
         )
@@ -363,7 +629,6 @@
             [grad_gate.reshape(-1, DI), grad_conv.reshape(-1, CH), grad_raw.reshape(-1, HEADS)],
             axis=1,
         ).astype(jnp.bfloat16)
-        grad_in_weight = contract_rows(normed_low, grad_projected)
         grad_normed = contract_cols(grad_projected, in_weight)
         grad_rows, grad_norm_gain = norm_back(grad_normed)
         input_grads.append(
@@ -373,28 +638,35 @@
         )
         current = (
             grad_norm_gain,
-            grad_in_weight,
             grad_kernel,
             grad_shift,
             grad_stepb,
             grad_decay,
             grad_skips,
             grad_gains,
-            grad_out_weight,
-        )
+        )
+        factors.append((normed_low, grad_projected, gated_low, upstream))
         totals = current if totals is None else jax.tree.map(jnp.add, totals, current)
-    flat_len = master.shape[0] * lax.axis_size(DP)
-    flat = jnp.concatenate(
-        [piece.reshape(-1) for piece in totals] + [jnp.zeros((flat_len - NPARAM,), jnp.float32)]
-    )
-    quarter = sum_in_tiles(flat, DP_GROUP, 0)
-    shard = collect(quarter, "group", 0)
+    normed_low, grad_projected, gated_low, upstream = (jnp.concatenate(part) for part in zip(*factors))
+    left = normed_low.T.reshape(D // 4, 4, -1).transpose(1, 0, 2)
+    right = jnp.pad(grad_projected, ((0, 0), (0, 4608 - grad_projected.shape[1])))
+    turned = jnp.concatenate([upstream[:, 32:], upstream[:, :32]], axis=1)
+    middle = jnp.concatenate([piece.reshape(-1) for piece in totals[1:]] + [jnp.zeros((32 + 5 * LANES,), jnp.float32)])
+    spot = position()
+    packed = pack(spot, left, right, gated_low.T, turned, totals[0].reshape(-1, LANES), middle.reshape(-1, LANES))
+    piece = reduce_pieces(packed[:3], packed[3:])
+    window = lax.all_gather(piece, GROUP, axis=0, tiled=True)
+    skew = (12 * lax.axis_index("x")) % 16
+    shard = lax.dynamic_slice(window, (skew, 0), (SHARD_LINES, LANES)).reshape(-1)
     squares = over_copies(jnp.sum(shard * shard), DP)
     clip_factor = MAX_NORM / jnp.maximum(jnp.sqrt(squares), MAX_NORM)
     first_moment, second_moment, updated = adam_update(
         shard * clip_factor, master, moment_one, moment_two, step_count
     )
-    copies = spread_gather(updated.astype(jnp.bfloat16), DP, 0)
+    blank = jnp.zeros_like(window)
+    placed = low(lax.dynamic_update_slice(blank, updated.reshape(SHARD_LINES, LANES), (skew, 0)))
+    mine = lax.dynamic_slice(placed, (PIECE * lax.axis_index(GROUP), 0), (PIECE, LANES))
+    copies = unpack(spot, gather_pieces(mine)).reshape(-1)
     return (
         jnp.stack(outputs),
         jnp.stack(input_grads),
@@ -407,16 +679,14 @@
 
 
 def solution(mesh):
-    finer = Mesh(
-        mesh.devices.reshape(4, 2, 4, mesh.shape["group"]), ("dp_0", "dp_1", "dp_2", "group")
-    )
+    finer = Mesh(mesh.devices.reshape(4, 2, 4, 2, 2), ("y", "zl", "x", "zh", "core"))
     return jax.shard_map(
         shards,
         mesh=finer,
         in_specs=(
-            P(None, DP, "group", None),
+            P(None, DP, GROUP, None),
             P(None, DP, None),
-            P(None, DP, "group", None),
+            P(None, DP, GROUP, None),
             P(),
             P(),
             P(),
@@ -432,8 +702,8 @@
             P(),
         ),
         out_specs=(
-            P(None, DP, "group", None),
-            P(None, DP, "group", None),
+            P(None, DP, GROUP, None),
+            P(None, DP, GROUP, None),
             P(DP),
             P(DP),
             P(DP),

time: 1590 us -> 836 us (0.53)
  local copies, waits for them, and re-layouts: 589 us -> 132 us
  waiting for transfers between devices: 558 us -> 105 us
  Pallas kernels: 0 us -> 81.9 us
  starting transfers between devices: 34.7 us -> 98.8 us
  other arithmetic: 160 us -> 203 us
  matrix products: 183 us -> 153 us
    unnamed x18 -> x4, waiting for transfers between devices: 346 us -> 0.07 us
    concatenate x2 -> x3, local copies, waits for them, and re-layouts: 235 us -> 1.53 us  [the longest x1 1.47 us: shards(): jnp.concatenate([piece.reshape(-1) for piece in totals[1:]] + [jnp.zeros(...]
    all_gather x6 -> x0, waiting for transfers between devices: 197 us -> none  [gather_in_order(): parts = lax.all_gather(parts, axes[k], axis=0, tiled=True)]
    ppermute x0 -> x57, waiting for transfers between devices: none -> 97.6 us  [the longest x21 47.1 us: from_offset(): return lax.ppermute(block, RING[axis], route)]
    reshape x9 -> x3, local copies, waits for them, and re-layouts: 95.7 us -> 6.02 us  [the longest x2 4.64 us: shards(): left = normed_low.T.reshape(D // 4, 4, -1).transpose(1, 0, 2)]
    pallas_call x0 -> x2, Pallas kernels: none -> 81.9 us  [the longest x1 65.2 us: pack(): pl.pallas_call(pack_kernel, out_shape=shapes + shapes, in_specs=[pl.Block...]
    ppermute x0 -> x57, starting transfers between devices: none -> 78.3 us  [the longest x21 35.3 us: to_offset(): return lax.ppermute(block, RING[axis], route)]
    unnamed x390 -> x338, local copies, waits for them, and re-layouts: 100 us -> 22.9 us
  transfers between devices with their start and end apart: 20 -> 66, of which waited for: 12 -> 24; matrix products, arithmetic and copies ran while one was open for 21% -> 27% of each run, Pallas kernels for 0% -> 0%
where the time goes in v1:
time: 836 us; the launch traced here: 823 us
  other arithmetic  203 us (24%)
  matrix products  153 us (18%)
  local copies, waits for them, and re-layouts  132 us (16%)
  waiting for transfers between devices  105 us (13%)
  starting transfers between devices  98.8 us (12%)
  Pallas kernels  81.9 us (10%)
  blocking collectives  27.7 us (3%)
  between operations  20.7 us (2%)
    dot_general x6, matrix products, mix_out(): jnp.einsum('ijh,ij,jhp->ihp', kernel, intersection, inflow, precision=HIG...  66.8 us
    pallas_call x1, Pallas kernels, pack(): pl.pallas_call(pack_kernel, out_shape=shapes + shapes, in_specs=[pl.Block...  65.2 us
    ppermute x21, waiting for transfers between devices, from_offset(): return lax.ppermute(block, RING[axis], route)  47.1 us
    ppermute x21, waiting for transfers between devices, to_offset(): return lax.ppermute(block, RING[axis], route)  45.2 us
    ppermute x21, starting transfers between devices, to_offset(): return lax.ppermute(block, RING[axis], route)  35.3 us
    select_n x12, other arithmetic, step(): jnp.where(position < mine, new, old)  31.3 us
    concatenate x2, other arithmetic, shards(): jnp.concatenate(part)  26.1 us
    ppermute x21, starting transfers between devices, from_offset(): return lax.ppermute(block, RING[axis], route)  24.3 us
  transfers between devices with their start and end apart: 66, of which 24 were waited for; matrix products, arithmetic and copies ran while one was open for 27% of the time, Pallas kernels for 0%

profile of v1, /device:TPU:1, one launch (start us, length us, event | category | flops | bytes accessed | tf_op | source)
XLA Modules:
  0.0 823.1 jit_solution(1213203738750617508)
XLA Ops:
  11.5 6.5 fusion.255
  21.8 6.9 collective-permute-start.1
  28.8 6.1 fusion.254
  111.1 8.1 all_gather.42
  119.2 6.6 all_gather.39
  137.8 9.7 %while.57 = (s32[]{:T(128)}, f32[1,32,64,128]{3,2,1,0:T(8,128)}, s32[]{:T(128)}, f32[4,1,32]{2,1,0:T(1,128)}, f32[4,1,32,64,128]{4,3,2,1,0:T(8,128)}, /*index=5*/s32[]{:T(128)}, s32[]{:T(128)}) while((s32[]{:T(128)}, f32[1,32,64,128]{3,2,1,0:T(8,128)}, s32[]{:T(128)}, f32[4,1,32]{2,1,0:T(1,128)}, ...), condition=%wide.region_10.12_spmd.clone, body=%wide.region_9.11_spmd.clone.sunk | while | flops 1048580 | bytes 3146225 | solution.py:51
  151.9 9.8 %while.56 = (s32[]{:T(128)}, f32[1,32,64,128]{3,2,1,0:T(8,128)}, s32[]{:T(128)}, f32[4,1,32]{2,1,0:T(1,128)}, f32[4,1,32,64,128]{4,3,2,1,0:T(8,128)}, /*index=5*/s32[]{:T(128)}, s32[]{:T(128)}) while((s32[]{:T(128)}, f32[1,32,64,128]{3,2,1,0:T(8,128)}, s32[]{:T(128)}, f32[4,1,32]{2,1,0:T(1,128)}, f32[4,1,32,64,128]{4,3,2,1,0:T(8,128)}, ...), condition=%wide.region_4.6_spmd.clone, body=%wide.region_3.5_spmd.clone.sunk | while | flops 1048580 | bytes 3146225 | solution.py:51
  165.1 12.8 %bitcast_add_fusion.6 = f32[1,256,32,64]{1,3,2,0:T(8,128)S(1)} fusion(f32[256,32,64]{0,2,1:T(8,128)} %fusion.152, f32[256,32,64]{0,2,1:T(8,128)S(1)} %bitcast.730, f32[256,256]{1,0:T(8,128)S(1)} %copy-done.70, f32[256,32]{0,1:T(8,128)S(1)} %copy-done.99, pred[256,256]{1,0:T(8,128)(4,1)S(1)} %copy-done.90, f32[256,32]{0,1:T(8,128)S(1)} %copy-done.85), kind=kOutput, calls=%fused_computation.139 | convolution fusion | flops 1620049920 | bytes 6684672 | tf_op jit(solution)/shard_map/jvp(vmap(ijh,ij,jhp->ihp))/dot_general | solution.py:431
  178.0 10.1 %bitcast_add_fusion.7 = f32[1,256,32,64]{1,3,2,0:T(8,128)S(1)} fusion(f32[256,32,64]{0,2,1:T(8,128)S(1)} %fusion.155, f32[256,32,64]{0,2,1:T(8,128)S(1)} %bitcast.735, f32[256,256]{1,0:T(8,128)S(1)} %copy-done.72, f32[256,32]{0,1:T(8,128)S(1)} %copy-done.101, pred[256,256]{1,0:T(8,128)(4,1)S(1)} %copy-done.92, f32[256,32]{0,1:T(8,128)S(1)} %copy-done.86), kind=kOutput, calls=%fused_computation.140 | convolution fusion | flops 1620049920 | bytes 6684672 | tf_op jit(solution)/shard_map/jvp(vmap(ijh,ij,jhp->ihp))/dot_general | solution.py:431
  242.1 14.7 %fusion.25 = (f32[256,32]{0,1:T(8,128)}, f32[256,32]{0,1:T(8,128)}, f32[256,256]{1,0:T(8,128)}) fusion(f32[256,256]{1,0:T(8,128)} %fusion.188, f32[256,32]{0,1:T(8,128)} %copy.370, pred[256,256]{1,0:T(8,128)(4,1)} %convert_compare_fusion.1, f32[32,256,64]{1,2,0:T(8,128)} %bitcast.738, f32[256,32,64]{0,2,1:T(8,128)} %bitcast.733), kind=kOutput, calls=%fused_computation.35 | convolution fusion | flops 1633599488 | bytes 4882432 | tf_op jit(solution)/shard_map/transpose(jvp(vmap(ijh,ij,jhp->ihp)))/dot_general | solution.py:431
  259.8 14.8 %fusion.27 = (f32[256,32]{0,1:T(8,128)}, f32[256,32]{0,1:T(8,128)}, f32[256,256]{1,0:T(8,128)}) fusion(f32[256,256]{1,0:T(8,128)} %fusion.183, f32[256,32]{0,1:T(8,128)} %copy.382, pred[256,256]{1,0:T(8,128)(4,1)} %convert_compare_fusion, f32[32,256,64]{1,2,0:T(8,128)} %bitcast.725, f32[256,32,64]{0,2,1:T(8,128)} %bitcast.728), kind=kOutput, calls=%fused_computation.37 | convolution fusion | flops 1633599488 | bytes 4882432 | tf_op jit(solution)/shard_map/transpose(jvp(vmap(ijh,ij,jhp->ihp)))/dot_general | solution.py:431
  300.4 9.7 %while.58 = (s32[]{:T(128)}, f32[1,32,64,128]{3,2,1,0:T(8,128)}, s32[]{:T(128)}, f32[4,1,32,64,128]{4,3,2,1,0:T(8,128)}, f32[4,1,32]{2,1,0:T(1,128)}, /*index=5*/s32[]{:T(128)}, s32[]{:T(128)}) while((s32[]{:T(128)}, f32[1,32,64,128]{3,2,1,0:T(8,128)}, s32[]{:T(128)}, f32[4,1,32,64,128]{4,3,2,1,0:T(8,128)}, ...), condition=%wide.region_14.16_spmd.clone, body=%wide.region_13.15_spmd.clone.sunk | while | flops 1048580 | bytes 3146225 | solution.py:51
  322.8 10.1 %while.59 = (s32[]{:T(128)}, f32[1,32,64,128]{3,2,1,0:T(8,128)}, s32[]{:T(128)}, f32[4,1,32,64,128]{4,3,2,1,0:T(8,128)}, f32[4,1,32]{2,1,0:T(1,128)}, /*index=5*/s32[]{:T(128)}, s32[]{:T(128)}) while((s32[]{:T(128)}, f32[1,32,64,128]{3,2,1,0:T(8,128)}, s32[]{:T(128)}, f32[4,1,32,64,128]{4,3,2,1,0:T(8,128)}, ...), condition=%wide.region_26.28_spmd.clone, body=%wide.region_25.27_spmd.clone.sunk | while | flops 1048580 | bytes 3146225 | solution.py:51
  341.9 7.2 bitcast_add_fusion.5
  351.5 7.2 bitcast_add_fusion.4
  361.7 6.2 multiply_reduce_fusion.3
  460.6 6.3 fusion.62
  467.0 25.4 %maximum_maximum_fusion = bf16[512,4384]{0,1:T(8,128)(2,1)} fusion(bf16[256,32]{0,1:T(8,128)(2,1)S(1)} %bitcast.772, bf16[256,2304]{0,1:T(8,128)(2,1)S(1)} %copy-done.35, bf16[256,2048]{0,1:T(8,128)(2,1)S(1)} %copy-done.38, bf16[256,32]{0,1:T(8,128)(2,1)S(1)} %bitcast.769, bf16[256,2304]{0,1:T(8,128)(2,1)S(1)} %fusion.114, bf16[256,2048]{0,1:T(8,128)(2,1)S(1)} %copy-done.44), kind=kLoop, calls=%fused_computation.40 | loop fusion | flops 26935296 | bytes 8978432 | tf_op jit(solution)/shard_map/concatenate | solution.py:650
  496.5 6.5 copy.472
  508.5 65.2 %pack_gradients.1 = (bf16[9216,128]{1,0:T(8,128)(2,1)}, bf16[9216,128]{1,0:T(8,128)(2,1)}, bf16[8192,128]{1,0:T(8,128)(2,1)}, bf16[9216,128]{1,0:T(8,128)(2,1)},...) custom-call(s32[4]{0:T(128)} %pad_add_fusion.4.pos, bf16[4,256,512]{2,1,0:T(8,128)(2,1)} %bitcast.762, ...), custom_call_target="tpu_custom_call" | custom-call | flops 7000000000 | bytes 25000000 | tf_op jit(solution)/shard_map/pack_gradients/pallas_call | solution.py:192
  590.8 6.7 collective-permute-done.16
  600.2 7.5 collective-permute-done.18
  624.9 9.5 %collective-permute-done.10 = bf16[2304,128]{1,0:T(8,128)(2,1)S(1)} collective-permute-done((bf16[2304,128]{1,0:T(8,128)(2,1)S(1)}, bf16[2304,128]{1,0:T(8,128)(2,1)S(1)}, u32[]{:S(2)}, u32[]{:S(2)}) %collective-permute-start.10) | collective-permute-done | bytes 589856 | tf_op jit(solution)/shard_map/ppermute | solution.py:247
  646.0 7.2 collective-permute-done.13
  665.0 13.1 %all_gather.49 = f32[1664,128]{1,0:T(8,128)S(1)} all-gather(f32[416,128]{1,0:T(8,128)S(1)} %pad_maximum_fusion.6), channel_id=1, replica_groups=mesh['y'=4,'zl'=2,'x'=4,'zh'=2,'core'=2] {'zh','core'}, dimensions={0}, use_global_device_ids=true | all-gather | bytes 1064960 | tf_op jit(solution)/shard_map/all_gather | solution.py:658
  680.1 6.9 all-to-all-start
  687.0 7.1 all-to-all-done
  725.3 6.3 collective-permute-start.53
  735.4 10.9 %collective-permute-done.48.rest_11_ = bf16[2048,128]{1,0:T(8,128)(2,1)S(1)} collective-permute-done((bf16[2048,128]{1,0:T(8,128)(2,1)S(1)}, bf16[2048,128]{1,0:T(8,128)(2,1)S(1)}, u32[]{:S(2)}, u32[]{:S(2)}) %collective-permute-start.48) | collective-permute-done | bytes 524320 | tf_op jit(solution)/shard_map/ppermute | solution.py:85
  749.2 9.1 %collective-permute-done.47.rest_10_ = bf16[2048,128]{1,0:T(8,128)(2,1)S(1)} collective-permute-done((bf16[2048,128]{1,0:T(8,128)(2,1)S(1)}, bf16[2048,128]{1,0:T(8,128)(2,1)S(1)}, u32[]{:S(2)}, u32[]{:S(2)}) %collective-permute-start.47) | collective-permute-done | bytes 524320 | tf_op jit(solution)/shard_map/ppermute | solution.py:85
  776.1 14.8 %collective-permute-done.39.rest_3_ = bf16[2304,128]{1,0:T(8,128)(2,1)S(1)} collective-permute-done((bf16[2304,128]{1,0:T(8,128)(2,1)S(1)}, bf16[2304,128]{1,0:T(8,128)(2,1)S(1)}, u32[]{:S(2)}, u32[]{:S(2)}) %collective-permute-start.39) | collective-permute-done | bytes 589856 | tf_op jit(solution)/shard_map/ppermute | solution.py:85
  799.7 16.7 %unpack_weights.1 = bf16[51584,128]{1,0:T(8,128)(2,1)} custom-call(s32[4]{0:T(128)S(1)} %copy-done, bf16[2304,128]{1,0:T(8,128)(2,1)S(1)} %get-tuple-element.734.rest_0_, bf16[2304,128]{1,0:T(8,128)(2,1)S(1)} %collective-permute-done.37.rest_1_, bf16[2304,128]{1,0:T(8,128)(2,1)S(1)} %collective-permute-done.38.rest_2_, ...), custom_call_target="tpu_custom_call" | custom-call | bytes 27000000 | tf_op jit(solution)/shard_map/unpack_weights/pallas_call | solution.py:369
  (723 shorter events, 475.8 us)
Async XLA Ops:
  7.2 130.6 %all-gather.11.cloned.1.call-start = ((), (), s32[]{:S(2)}) async-start(), calls=%async_computation.2 | async-start | bytes 5242880 | tf_op jit(solution)/shard_map/all_gather | solution.py:39
  21.8 28.6 %collective-permute-start.1 = (bf16[1,3,2304]{2,1,0:T(4,128)(2,1)S(1)}, bf16[1,3,2304]{2,1,0:T(4,128)(2,1)S(1)}, u32[]{:S(2)}, u32[]{:S(2)}) collective-permute-start(bf16[1,3,2304]{2,1,0:T(4,128)(2,1)S(1)} %copy.384), channel_id=1, source_target_pairs={{0,1},{1,2},{2,3},{4,5},{5,6},{6,7},{8,9},{9,10},{10,11},{12,13},{... | collective-permute-start | bytes 41480 | tf_op jit(solution)/shard_map/ppermute | solution.py:34
  63.7 88.3 %all-gather.9.cloned.1.call-start = ((), (), s32[]{:S(2)}) async-start(), calls=%async_computation.1 | async-start | bytes 5242880 | tf_op jit(solution)/shard_map/all_gather | solution.py:39
  69.5 19.4 %collective-permute-start = (bf16[1,3,2304]{2,1,0:T(4,128)(2,1)}, bf16[1,3,2304]{2,1,0:T(4,128)(2,1)}, u32[]{:S(2)}, u32[]{:S(2)}) collective-permute-start(bf16[1,3,2304]{2,1,0:T(4,128)(2,1)} %copy.372), channel_id=1, source_target_pairs={{0,1},{1,2},{2,3},{4,5},{5,6},{6,7},{8,9},{9,10},{10,11},{12,13},{... | collective-permute-start | bytes 41480 | tf_op jit(solution)/shard_map/ppermute | solution.py:34
  103.2 192.4 %all-gather.13.cloned.1.call-start = ((), (), s32[]{:S(2)}) async-start(), calls=%async_computation.3 | async-start | bytes 5242880 | tf_op jit(solution)/shard_map/all_gather | solution.py:39
  208.0 109.9 %all-gather.15.cloned.1.call-start = ((), (), s32[]{:S(2)}) async-start(), calls=%async_computation.4 | async-start | bytes 5242880 | tf_op jit(solution)/shard_map/all_gather | solution.py:39
  433.8 17.3 %collective-permute-start.3 = (f32[1,3,2304]{2,0,1:T(1,128)}, f32[1,3,2304]{2,0,1:T(1,128)}, u32[]{:S(2)}, u32[]{:S(2)}) collective-permute-start(f32[1,3,2304]{2,0,1:T(1,128)} %copy.413), channel_id=1, source_target_pairs={{1,0},{2,1},{3,2},{5,4},{6,5},{7,6},{9,8},{10,9},{11,10},{13,12},{... | collective-permute-start | bytes 82952 | tf_op jit(solution)/shard_map/ppermute | solution.py:34
  438.2 18.1 %collective-permute-start.2 = (f32[1,3,2304]{2,0,1:T(1,128)}, f32[1,3,2304]{2,0,1:T(1,128)}, u32[]{:S(2)}, u32[]{:S(2)}) collective-permute-start(f32[1,3,2304]{2,0,1:T(1,128)} %copy.398), channel_id=1, source_target_pairs={{1,0},{2,1},{3,2},{5,4},{6,5},{7,6},{9,8},{10,9},{11,10},{13,12},{... | collective-permute-start | bytes 82952 | tf_op jit(solution)/shard_map/ppermute | solution.py:34
  581.2 16.3 %collective-permute-start.16 = (bf16[2048,128]{1,0:T(8,128)(2,1)S(1)}, bf16[2048,128]{1,0:T(8,128)(2,1)S(1)}, u32[]{:S(2)}, u32[]{:S(2)}) collective-permute-start(bf16[2048,128]{1,0:T(8,128)(2,1)S(1)} %get-tuple-element.711), channel_id=1, source_target_pairs={{0,16},{16,2},{2,18},{18,0},{1,17},{17,3},{3,19},{19,1},{4,20},{20... | collective-permute-start | bytes 1572872 | tf_op jit(solution)/shard_map/ppermute | solution.py:247
  582.2 25.5 %collective-permute-start.18 = (bf16[2048,128]{1,0:T(8,128)(2,1)S(1)}, bf16[2048,128]{1,0:T(8,128)(2,1)S(1)}, u32[]{:S(2)}, u32[]{:S(2)}) collective-permute-start(bf16[2048,128]{1,0:T(8,128)(2,1)S(1)} %get-tuple-element.712), channel_id=1, source_target_pairs={{0,18},{16,0},{2,16},{18,2},{1,19},{17,1},{3,17},{19,3},{4,22},{20... | collective-permute-start | bytes 1572872 | tf_op jit(solution)/shard_map/ppermute | solution.py:247
  585.4 24.3 %collective-permute-start.17 = (bf16[2048,128]{1,0:T(8,128)(2,1)S(1)}, bf16[2048,128]{1,0:T(8,128)(2,1)S(1)}, u32[]{:S(2)}, u32[]{:S(2)}) collective-permute-start(bf16[2048,128]{1,0:T(8,128)(2,1)S(1)} %get-tuple-element.713), channel_id=1, source_target_pairs={{0,2},{16,18},{2,0},{18,16},{1,3},{17,19},{3,1},{19,17},{4,6},{20,... | collective-permute-start | bytes 1572872 | tf_op jit(solution)/shard_map/ppermute | solution.py:247
  587.3 25.3 %collective-permute-start.5 = (bf16[2304,128]{1,0:T(8,128)(2,1)S(1)}, bf16[2304,128]{1,0:T(8,128)(2,1)S(1)}, u32[]{:S(2)}, u32[]{:S(2)}) collective-permute-start(bf16[2304,128]{1,0:T(8,128)(2,1)S(1)} %get-tuple-element.693), channel_id=1, source_target_pairs={{0,4},{4,8},{8,12},{12,0},{1,5},{5,9},{9,13},{13,1},{2,6},{6,10},{... | collective-permute-start | bytes 1769480 | tf_op jit(solution)/shard_map/ppermute | solution.py:247
  588.5 24.6 %collective-permute-start.7 = (bf16[2304,128]{1,0:T(8,128)(2,1)S(1)}, bf16[2304,128]{1,0:T(8,128)(2,1)S(1)}, u32[]{:S(2)}, u32[]{:S(2)}) collective-permute-start(bf16[2304,128]{1,0:T(8,128)(2,1)S(1)} %get-tuple-element.694), channel_id=1, source_target_pairs={{0,12},{4,0},{8,4},{12,8},{1,13},{5,1},{9,5},{13,9},{2,14},{6,2},{... | collective-permute-start | bytes 1769480 | tf_op jit(solution)/shard_map/ppermute | solution.py:247
  597.5 18.6 %collective-permute-start.6 = (bf16[2304,128]{1,0:T(8,128)(2,1)S(1)}, bf16[2304,128]{1,0:T(8,128)(2,1)S(1)}, u32[]{:S(2)}, u32[]{:S(2)}) collective-permute-start(bf16[2304,128]{1,0:T(8,128)(2,1)S(1)} %get-tuple-element.695), channel_id=1, source_target_pairs={{0,8},{4,12},{8,0},{12,4},{1,9},{5,13},{9,1},{13,5},{2,10},{6,14},... | collective-permute-start | bytes 1769480 | tf_op jit(solution)/shard_map/ppermute | solution.py:247
  607.7 15.7 %collective-permute-start.9 = (bf16[2304,128]{1,0:T(8,128)(2,1)S(1)}, bf16[2304,128]{1,0:T(8,128)(2,1)S(1)}, u32[]{:S(2)}, u32[]{:S(2)}) collective-permute-start(bf16[2304,128]{1,0:T(8,128)(2,1)S(1)} %get-tuple-element.696), channel_id=1, source_target_pairs={{0,32},{32,64},{64,96},{96,0},{1,33},{33,65},{65,97},{97,1},{2,34}... | collective-permute-start | bytes 1769480 | tf_op jit(solution)/shard_map/ppermute | solution.py:247
  612.6 21.8 %collective-permute-start.10 = (bf16[2304,128]{1,0:T(8,128)(2,1)S(1)}, bf16[2304,128]{1,0:T(8,128)(2,1)S(1)}, u32[]{:S(2)}, u32[]{:S(2)}) collective-permute-start(bf16[2304,128]{1,0:T(8,128)(2,1)S(1)} %get-tuple-element.698), channel_id=1, source_target_pairs={{0,64},{32,96},{64,0},{96,32},{1,65},{33,97},{65,1},{97,33},{2,66}... | collective-permute-start | bytes 1769480 | tf_op jit(solution)/shard_map/ppermute | solution.py:247
  613.1 28.8 %collective-permute-start.19 = (bf16[512,128]{1,0:T(8,128)(2,1)S(1)}, bf16[512,128]{1,0:T(8,128)(2,1)S(1)}, u32[]{:S(2)}, u32[]{:S(2)}) collective-permute-start(bf16[512,128]{1,0:T(8,128)(2,1)S(1)} %get-tuple-element.730), channel_id=1, source_target_pairs={{0,4},{4,8},{8,12},{12,0},{1,5},{5,9},{9,13},{13,1},{2,6},{6,10},{... | collective-permute-start | bytes 393224 | tf_op jit(solution)/shard_map/ppermute | solution.py:247
  616.0 27.7 %collective-permute-start.21 = (bf16[512,128]{1,0:T(8,128)(2,1)S(1)}, bf16[512,128]{1,0:T(8,128)(2,1)S(1)}, u32[]{:S(2)}, u32[]{:S(2)}) collective-permute-start(bf16[512,128]{1,0:T(8,128)(2,1)S(1)} %get-tuple-element.731), channel_id=1, source_target_pairs={{0,12},{4,0},{8,4},{12,8},{1,13},{5,1},{9,5},{13,9},{2,14},{6,2},{... | collective-permute-start | bytes 393224 | tf_op jit(solution)/shard_map/ppermute | solution.py:247
  623.4 20.4 %collective-permute-start.20 = (bf16[512,128]{1,0:T(8,128)(2,1)S(1)}, bf16[512,128]{1,0:T(8,128)(2,1)S(1)}, u32[]{:S(2)}, u32[]{:S(2)}) collective-permute-start(bf16[512,128]{1,0:T(8,128)(2,1)S(1)} %get-tuple-element.732), channel_id=1, source_target_pairs={{0,8},{4,12},{8,0},{12,4},{1,9},{5,13},{9,1},{13,5},{2,10},{6,14},... | collective-permute-start | bytes 393224 | tf_op jit(solution)/shard_map/ppermute | solution.py:247
  717.1 18.3 %collective-permute-start.57 = (bf16[2048,128]{1,0:T(8,128)(2,1)S(1)}, bf16[2048,128]{1,0:T(8,128)(2,1)S(1)}, u32[]{:S(2)}, u32[]{:S(2)}) collective-permute-start(bf16[2048,128]{1,0:T(8,128)(2,1)S(1)} %constant_dynamic-update-slice_fusion.16.rest_8_), channel_id=1, source_target_pairs={{0,1},{1,0},{2,3},{3,2},{4,5},{5,4},{6,7},{7,6},{8,9},{9,8},{10,11... | collective-permute-start | bytes 1572872 | tf_op jit(solution)/shard_map/ppermute | solution.py:89
  725.3 36.8 %collective-permute-start.53 = (bf16[2304,128]{1,0:T(8,128)(2,1)S(1)}, bf16[2304,128]{1,0:T(8,128)(2,1)S(1)}, u32[]{:S(2)}, u32[]{:S(2)}) collective-permute-start(bf16[2304,128]{1,0:T(8,128)(2,1)S(1)} %get-tuple-element.733.rest_4_), channel_id=1, source_target_pairs={{0,1},{1,0},{2,3},{3,2},{4,5},{5,4},{6,7},{7,6},{8,9},{9,8},{10,11... | collective-permute-start | bytes 1769480 | tf_op jit(solution)/shard_map/ppermute | solution.py:89
  731.6 30.6 %collective-permute-start.42 = (bf16[2304,128]{1,0:T(8,128)(2,1)S(1)}, bf16[2304,128]{1,0:T(8,128)(2,1)S(1)}, u32[]{:S(2)}, u32[]{:S(2)}) collective-permute-start(bf16[2304,128]{1,0:T(8,128)(2,1)S(1)} %get-tuple-element.733.rest_4_), channel_id=1, source_target_pairs={{96,0},{0,32},{32,64},{64,96},{97,1},{1,33},{33,65},{65,97},{98,2}... | collective-permute-start | bytes 1769480 | tf_op jit(solution)/shard_map/ppermute | solution.py:85
  732.4 25.9 %collective-permute-start.47 = (bf16[2048,128]{1,0:T(8,128)(2,1)S(1)}, bf16[2048,128]{1,0:T(8,128)(2,1)S(1)}, u32[]{:S(2)}, u32[]{:S(2)}) collective-permute-start(bf16[2048,128]{1,0:T(8,128)(2,1)S(1)} %constant_dynamic-update-slice_fusion.16.rest_8_), channel_id=1, source_target_pairs={{2,0},{18,16},{0,2},{16,18},{3,1},{19,17},{1,3},{17,19},{6,4},{22,... | collective-permute-start | bytes 1572872 | tf_op jit(solution)/shard_map/ppermute | solution.py:85
  735.4 25.3 %collective-permute-start.46 = (bf16[2048,128]{1,0:T(8,128)(2,1)S(1)}, bf16[2048,128]{1,0:T(8,128)(2,1)S(1)}, u32[]{:S(2)}, u32[]{:S(2)}) collective-permute-start(bf16[2048,128]{1,0:T(8,128)(2,1)S(1)} %constant_dynamic-update-slice_fusion.16.rest_8_), channel_id=1, source_target_pairs={{16,0},{2,16},{18,2},{0,18},{17,1},{3,17},{19,3},{1,19},{20,4},{6,... | collective-permute-start | bytes 1572872 | tf_op jit(solution)/shard_map/ppermute | solution.py:85
  746.3 20.7 %collective-permute-start.41 = (bf16[2304,128]{1,0:T(8,128)(2,1)S(1)}, bf16[2304,128]{1,0:T(8,128)(2,1)S(1)}, u32[]{:S(2)}, u32[]{:S(2)}) collective-permute-start(bf16[2304,128]{1,0:T(8,128)(2,1)S(1)} %get-tuple-element.733.rest_4_), channel_id=1, source_target_pairs={{64,0},{96,32},{0,64},{32,96},{65,1},{97,33},{1,65},{33,97},{66,2}... | collective-permute-start | bytes 1769480 | tf_op jit(solution)/shard_map/ppermute | solution.py:85
  758.3 15.9 %collective-permute-start.40 = (bf16[2304,128]{1,0:T(8,128)(2,1)S(1)}, bf16[2304,128]{1,0:T(8,128)(2,1)S(1)}, u32[]{:S(2)}, u32[]{:S(2)}) collective-permute-start(bf16[2304,128]{1,0:T(8,128)(2,1)S(1)} %get-tuple-element.733.rest_4_), channel_id=1, source_target_pairs={{32,0},{64,32},{96,64},{0,96},{33,1},{65,33},{97,65},{1,97},{34,2}... | collective-permute-start | bytes 1769480 | tf_op jit(solution)/shard_map/ppermute | solution.py:85
  760.7 15.4 %collective-permute-start.49 = (bf16[2304,128]{1,0:T(8,128)(2,1)S(1)}, bf16[2304,128]{1,0:T(8,128)(2,1)S(1)}, u32[]{:S(2)}, u32[]{:S(2)}) collective-permute-start(bf16[2304,128]{1,0:T(8,128)(2,1)S(1)} %get-tuple-element.734.rest_0_), channel_id=1, source_target_pairs={{0,1},{1,0},{2,3},{3,2},{4,5},{5,4},{6,7},{7,6},{8,9},{9,8},{10,11... | collective-permute-start | bytes 1769480 | tf_op jit(solution)/shard_map/ppermute | solution.py:89
  762.1 28.7 %collective-permute-start.39 = (bf16[2304,128]{1,0:T(8,128)(2,1)S(1)}, bf16[2304,128]{1,0:T(8,128)(2,1)S(1)}, u32[]{:S(2)}, u32[]{:S(2)}) collective-permute-start(bf16[2304,128]{1,0:T(8,128)(2,1)S(1)} %get-tuple-element.734.rest_0_), channel_id=1, source_target_pairs={{12,0},{0,4},{4,8},{8,12},{13,1},{1,5},{5,9},{9,13},{14,2},{2,6},{... | collective-permute-start | bytes 1769480 | tf_op jit(solution)/shard_map/ppermute | solution.py:85
  762.2 29.6 %collective-permute-start.38 = (bf16[2304,128]{1,0:T(8,128)(2,1)S(1)}, bf16[2304,128]{1,0:T(8,128)(2,1)S(1)}, u32[]{:S(2)}, u32[]{:S(2)}) collective-permute-start(bf16[2304,128]{1,0:T(8,128)(2,1)S(1)} %get-tuple-element.734.rest_0_), channel_id=1, source_target_pairs={{8,0},{12,4},{0,8},{4,12},{9,1},{13,5},{1,9},{5,13},{10,2},{14,6},... | collective-permute-start | bytes 1769480 | tf_op jit(solution)/shard_map/ppermute | solution.py:85
  767.0 27.1 %collective-permute-start.37 = (bf16[2304,128]{1,0:T(8,128)(2,1)S(1)}, bf16[2304,128]{1,0:T(8,128)(2,1)S(1)}, u32[]{:S(2)}, u32[]{:S(2)}) collective-permute-start(bf16[2304,128]{1,0:T(8,128)(2,1)S(1)} %get-tuple-element.734.rest_0_), channel_id=1, source_target_pairs={{4,0},{8,4},{12,8},{0,12},{5,1},{9,5},{13,9},{1,13},{6,2},{10,6},{... | collective-permute-start | bytes 1769480 | tf_op jit(solution)/shard_map/ppermute | solution.py:85
  774.2 20.4 %collective-permute-start.60 = (bf16[2048,128]{1,0:T(8,128)(2,1)S(1)}, bf16[2048,128]{1,0:T(8,128)(2,1)S(1)}, u32[]{:S(2)}, u32[]{:S(2)}) collective-permute-start(bf16[2048,128]{1,0:T(8,128)(2,1)S(1)} %collective-permute-done.48.rest_11_), channel_id=1, source_target_pairs={{0,1},{1,0},{2,3},{3,2},{4,5},{5,4},{6,7},{7,6},{8,9},{9,8},{10,11... | collective-permute-start | bytes 1572872 | tf_op jit(solution)/shard_map/ppermute | solution.py:89
  776.1 18.6 %collective-permute-start.59 = (bf16[2048,128]{1,0:T(8,128)(2,1)S(1)}, bf16[2048,128]{1,0:T(8,128)(2,1)S(1)}, u32[]{:S(2)}, u32[]{:S(2)}) collective-permute-start(bf16[2048,128]{1,0:T(8,128)(2,1)S(1)} %collective-permute-done.47.rest_10_), channel_id=1, source_target_pairs={{0,1},{1,0},{2,3},{3,2},{4,5},{5,4},{6,7},{7,6},{8,9},{9,8},{10,11... | collective-permute-start | bytes 1572872 | tf_op jit(solution)/shard_map/ppermute | solution.py:89
  (196 other events, 1555.5 us)
Sparse Core Ops, SparseCore 0:
  63.8 37.9 all-gather.10
  104.0 38.2 all-gather.8
  208.1 38.8 all-gather.12
  248.6 37.8 all-gather.14

commit v2 on v1

v2 whole, which is shorter than its diff:
```python
import functools

import jax
import jax.numpy as jnp
from jax import lax
from jax.experimental import pallas as pl
from jax.experimental.pallas import tpu as pltpu
from jax.sharding import Mesh
from jax.sharding import PartitionSpec as P

D = 1024
DI = 2048
HEADS = 32
HDIM = 64
STATE = 128
CH = 2304
DP = ("y", "zl", "x")
GROUP = ("zh", "core")


EPSILON = 1e-05
BETA_ONE = 0.9
BETA_TWO = 0.95
ADAM_EPSILON = 1e-08
LEARN_RATE = 0.01
WEIGHT_DECAY = 0.1
MAX_NORM = 1.0


def sent_to_all(shard, axis):
    copies = jnp.broadcast_to(shard, (lax.axis_size(axis), *shard.shape))
    return lax.all_to_all(copies, axis, split_axis=0, concat_axis=0, tiled=True)


def over_copies(shard, axis):
    everything = sent_to_all(shard, axis)
    return jnp.sum(everything, axis=0)


def norm_piece(values, scaling):
    factor = lax.rsqrt(jnp.mean(values * values, axis=-1, keepdims=True) + EPSILON)
    return values * factor * scaling


def adam_update(clipped, master, moment_one, moment_two, step_count):
    first_moment = BETA_ONE * moment_one + (1.0 - BETA_ONE) * clipped
    second_moment = BETA_TWO * moment_two + (1.0 - BETA_TWO) * clipped * clipped
    step_real = step_count[0].astype(jnp.float32)
    first_hat = first_moment / (1.0 - jnp.power(BETA_ONE, step_real))
    second_hat = second_moment / (1.0 - jnp.power(BETA_TWO, step_real))
    updated = master - LEARN_RATE * (
        first_hat / (jnp.sqrt(second_hat) + ADAM_EPSILON) + WEIGHT_DECAY * master
    )
    return (first_moment, second_moment, updated)


LANES = 128
LINES = 51584
SHARD_LINES = 1612
IN_LINE = 8
MID_LINE = 35080
OUT_LINE = 35187
PIECE = 416
SLOTS = 16
PARTS = ((0, 144), (144, 144), (288, 128))
TAIL_LINES = 51632
GROUP_LINES = 137
RING = {"x": ("x",), "y": ("y",), "z": ("zl", "zh")}
ROUTES = (("x", "z", "y"), ("y", "z", "X"), ("z", "x", "y"))


def ring_place(axis, i):
    i = i % 4
    return (i % 2) * 2 + i // 2 if axis == "z" else i


def from_offset(block, axis, distance):
    route = [(ring_place(axis, i + distance), ring_place(axis, i)) for i in range(4)]
    return lax.ppermute(block, RING[axis], route)


def swap_cores(block):
    return lax.ppermute(block, "core", [(0, 1), (1, 0)])


def position():
    return jnp.stack([lax.axis_index("y"), lax.axis_index("zl"), lax.axis_index("x"), lax.axis_index("core")]).astype(jnp.int32)


def first_tile(shard):
    return (403 * shard) // 4


def pack_kernel(pos, left, grad_gate, grad_ci, grad_raw, gated, cot, gain_part, mid_part, *rest):
    keep, send = rest[:3], rest[3:6]
    flat, carry, edge, stage, sems = rest[6:]
    lane = lax.broadcasted_iota(jnp.int32, (256, LANES), 1)

    flat[0:IN_LINE, :] = gain_part[...]
    flat[MID_LINE : MID_LINE + 104, :] = mid_part[0:104, :]
    flat[MID_LINE + 104 : MID_LINE + 107, :] = mid_part[104:107, :]
    def put(tile, k, line):
        moved = pltpu.roll(tile, 32 * k, 1) if k else tile
        whole = jnp.where(lane < 32 * k, carry[k], moved) if k else moved
        flat[pl.ds(IN_LINE + 34 * k + line, 256, stride=GROUP_LINES), :] = whole
        carry[k] = moved

    def columns(block, line, tiles):
        product = nt(left[...], block)
        for k in range(4):
            for t in range(tiles):
                put(product[256 * k : 256 * (k + 1), t * LANES : (t + 1) * LANES], k, line + t)

    def from_gate(j, _):
        columns(grad_gate[pl.ds(pl.multiple_of(j * 512, 512), 512), :], 4 * j, 4)
        return 0

    def from_conv(j, _):
        columns(grad_ci[pl.ds(pl.multiple_of(j * 512, 512), 512), :], 16 + 4 * j, 4)
        return 0

    lax.fori_loop(0, 4, from_gate, 0)
    lax.fori_loop(0, 4, from_conv, 0)
    heads = []
    for k in range(1, 4):
        heads.append(flat[pl.ds(IN_LINE + 34 * k, 256, stride=GROUP_LINES), :])
    columns(jnp.concatenate([grad_ci[2048:2304, :], grad_raw[...]], axis=0), 32, 3)
    for k in range(1, 4):
        at = pl.ds(IN_LINE + 34 * k, 256, stride=GROUP_LINES)
        flat[at, :] = jnp.where(lane < 32 * k, flat[at, :], heads[k - 1])

    edge[0:8, :] = mid_part[99:107, :]

    def rows(b, _):
        block = gated[pl.ds(pl.multiple_of(b * 256, 256), 256), :]
        product = jnp.dot(block, cot[...], preferred_element_type=jnp.float32)
        start = OUT_LINE + 2048 * b
        for t in range(7):
            flat[pl.ds(start + t, 256, stride=8), :] = product[:, t * LANES : (t + 1) * LANES]
        last = product[:, 7 * LANES :]
        edge[8:264, :] = last
        flat[pl.ds(start - 1, 256, stride=8), :] = jnp.where(lane < 96, edge[7:263, :], last)
        edge[0:8, :] = edge[256:264, :]
        return 0

    lax.fori_loop(0, 8, rows, 0)
    low = lax.broadcasted_iota(jnp.int32, (1, LANES), 1) < 96
    flat[OUT_LINE + 16383 : TAIL_LINES, :] = jnp.zeros((TAIL_LINES - OUT_LINE - 16383, LANES), jnp.float32)
    flat[OUT_LINE + 16383 : OUT_LINE + 16384, :] = jnp.where(low, edge[7:8, :], 0.0)

    my_y, my_x, my_core = pos[0], pos[2], pos[3]

    def drain(slot):
        pltpu.make_async_copy(stage.at[slot], keep[0].at[pl.ds(0, PIECE)], sems.at[slot]).wait()

    def ship(i, _):
        slot = i % SLOTS

        @pl.when(i >= SLOTS)
        def _():
            drain(slot)

        shard, quarter = i // 4, i % 4
        line = 16 * first_tile(shard) + PIECE * quarter
        stage[slot] = flat[pl.ds(pl.multiple_of(line, 16), PIECE), :].astype(jnp.bfloat16)
        x, zl, y = shard % 4, (shard // 4) % 2, shard // 8
        core = quarter % 2
        off = {"y": (y - my_y + 4) % 4, "z": 2 * zl + quarter // 2, "x": (x - my_x + 4) % 4, "X": x}
        for p, (start, size) in enumerate(PARTS):
            a, b, c = (off[axis] for axis in ROUTES[p])
            to = pl.ds(pl.multiple_of(((a * 4 + b) * 4 + c) * size, 16), size)
            source = stage.at[slot, pl.ds(start, size)]

            @pl.when(core == my_core)
            def _():
                pltpu.make_async_copy(source, keep[p].at[to], sems.at[slot]).start()

            @pl.when(core != my_core)
            def _():
                pltpu.make_async_copy(source, send[p].at[to], sems.at[slot]).start()

        return 0

    lax.fori_loop(0, 128, ship, 0)
    for slot in range(SLOTS):
        drain(slot)


def pack(pos, left, grad_gate, grad_ci, grad_raw, gated, cot, gain_part, mid_part):
    vmem, hbm = pl.BlockSpec(memory_space=pltpu.VMEM), pl.BlockSpec(memory_space=pl.ANY)
    shapes = [jax.ShapeDtypeStruct((64 * size, LANES), jnp.bfloat16) for _, size in PARTS]
    return pl.pallas_call(
        pack_kernel,
        out_shape=shapes + shapes,
        in_specs=[pl.BlockSpec(memory_space=pltpu.SMEM)] + [vmem] * 8,
        out_specs=[hbm] * 6,
        scratch_shapes=[
            pltpu.VMEM((TAIL_LINES, LANES), jnp.float32),
            pltpu.VMEM((4, 256, LANES), jnp.float32),
            pltpu.VMEM((264, LANES), jnp.float32),
            pltpu.VMEM((SLOTS, PIECE, LANES), jnp.bfloat16),
            pltpu.SemaphoreType.DMA((SLOTS,)),
        ],
        compiler_params=pltpu.CompilerParams(vmem_limit_bytes=60 * 2**20),
        cost_estimate=pl.CostEstimate(flops=7_000_000_000, bytes_accessed=25_000_000, transcendentals=0),
        name="pack_gradients",
    )(pos, left, grad_gate, grad_ci, grad_raw, gated, cot, gain_part, mid_part)


def real(v):
    return v.astype(jnp.float32)


def low(v):
    return v.astype(jnp.bfloat16)


def to_offset(block, axis, distance):
    route = [(ring_place(axis, i), ring_place(axis, i + distance)) for i in range(4)]
    return lax.ppermute(block, RING[axis], route)


def exchange(blocks, axis):
    blocks = blocks.reshape(4, -1, LANES)
    return lax.all_to_all(blocks, RING[axis], split_axis=0, concat_axis=0, tiled=True)


def quarters(block):
    return block.reshape(4, -1, LANES)


def ring_sum(block, axis):
    block = quarters(block)
    half = block.shape[1] // 32 * 16
    a, b = to_offset(block[2, :half], axis, 1), to_offset(block[2, half:], axis, 3)
    one = jnp.concatenate([low(real(block[1, :half]) + real(a)), block[1, half:]])
    three = jnp.concatenate([block[3, :half], low(real(block[3, half:]) + real(b))])
    return real(block[0]) + real(to_offset(one, axis, 1)) + real(to_offset(three, axis, 3))


def direct_sum(block, axis):
    block = quarters(block)
    moved = [to_offset(block[d], axis, d) for d in (1, 3, 2)]
    return real(block[0]) + real(moved[0]) + real(moved[1]) + real(moved[2])


def exchange_sum(block, axis):
    return jnp.sum(real(exchange(block, axis)), axis=0)


def reduce_pieces(keep, send):
    held = [None] * 3
    for p in (2, 0, 1):
        held[p] = low(real(keep[p]) + real(swap_cores(send[p])))
    third = low(exchange_sum(held[2], "z"))
    first, second = low(ring_sum(held[0], "x")), low(ring_sum(held[1], "y"))
    both = jnp.concatenate([quarters(first), quarters(second)], axis=1)
    both, third = low(exchange_sum(both, "z")), low(direct_sum(third, "x"))
    n0, n2 = PARTS[0][1], PARTS[2][1]
    first, second = both[: 4 * n0], both[4 * n0 :]
    outer = jnp.concatenate([quarters(first), quarters(third)], axis=1)
    second, outer = exchange_sum(second, "x"), direct_sum(outer, "y")
    return jnp.concatenate([outer[:n0], second, outer[n0:]])


def gather_pieces(piece):
    def spread(block, axis):
        return [block] + [from_offset(block, axis, d) for d in (1, 3, 2)]

    def in_order(parts):
        return jnp.concatenate([parts[0], parts[1], parts[3], parts[2]])

    def exchanged(block, axis):
        return exchange(jnp.broadcast_to(block, (4, *block.shape)), axis)

    n0, n1, n2 = (size for _, size in PARTS)
    first, second, third = piece[:n0], piece[n0 : n0 + n1], piece[n0 + n1 :]
    second = exchanged(second, "x").reshape(-1, LANES)
    outer = spread(jnp.concatenate([first, third]), "y")
    first = in_order([block[:n0] for block in outer])
    third = in_order([block[n0:] for block in outer])
    both = exchanged(jnp.concatenate([first, second]), "z")
    third = in_order(spread(third, "x"))
    first = both[:, : 4 * n0].reshape(-1, LANES)
    second = both[:, 4 * n0 :].reshape(-1, LANES)
    third = exchanged(third, "z").reshape(-1, LANES)

    def ring(block, axis):
        right, left = from_offset(block, axis, 3), from_offset(block, axis, 1)
        return right, left

    around = [ring(first, "x"), ring(second, "y")]
    mine = []
    for block, axis, (right, left) in zip((first, second), "xy", around):
        half = block.shape[0] // 2
        mine += [block, right, left, from_offset(right[:half], axis, 3), from_offset(left[half:], axis, 1)]
    mine.append(third)
    return mine + [swap_cores(block) for block in mine]


def unpack_kernel(pos, *rest):
    sources, out = rest[:22], rest[22]
    tiles, sem = rest[23:]
    my_y, my_x, my_core = pos[0], pos[2], pos[3]

    def place(p, a, b, c, core):
        off = dict(zip(ROUTES[p], (a, b, c)))
        y = (my_y + off["y"]) % 4
        x = off["X"] if p == 1 else (my_x + off["x"]) % 4
        return (y * 2 + off["z"] // 2) * 4 + x, 2 * (off["z"] % 2) + core

    table = []
    for p in range(2):
        for far, array, start, end in ((0, 0, 0, 16), (3, 1, 0, 16), (1, 2, 0, 16), (2, 3, 0, 8), (2, 4, 8, 16)):
            table.append((p, far, 5 * p + array, start, end))
    table += [(2, far, 10, 0, 16) for far in range(4)]

    def copy(source, here, line, size):
        here, line = pl.multiple_of(here, 16), pl.multiple_of(line, 16)
        pltpu.make_async_copy(source.at[pl.ds(here, size)], out.at[pl.ds(line, size)], sem).start()

    for other in range(2):
        core = (my_core + other) % 2
        for p, far, array, begin, end in table:
            source = sources[11 * other + array]
            start, size = PARTS[p]

            def move(i, _, p=p, far=far, source=source, begin=begin, start=start, size=size, core=core):
                shard, quarter = place(p, far, i // 4, i % 4, core)
                line = 16 * first_tile(shard) + PIECE * quarter + start
                here = (i - begin + (16 * far if p == 2 else 0)) * size
                if p == 0:

                    @pl.when(quarter == 0)
                    def _():
                        copy(source, here + 16, line + 16, size - 16)
                        pltpu.make_async_copy(
                            source.at[pl.ds(pl.multiple_of(here, 16), 16)], tiles.at[0, shard], sem
                        ).start()

                    @pl.when(quarter != 0)
                    def _():
                        copy(source, here, line, size)

                elif p == 1:
                    copy(source, here, line, size)
                else:

                    @pl.when(quarter == 3)
                    def _():
                        copy(source, here, line, 80)
                        x = shard % 4
                        skip = jnp.where((x == 1) | (x == 2), 80, 64)
                        pltpu.make_async_copy(
                            source.at[pl.ds(pl.multiple_of(here + skip, 16), 16)], tiles.at[1, shard], sem
                        ).start()

                    @pl.when(quarter != 3)
                    def _():
                        copy(source, here, line, size)

                return 0

            lax.fori_loop(begin, end, move, 0)
    moved = 128 * PIECE - 32 * 16 - 32 * 48
    pltpu.make_async_copy(out.at[pl.ds(0, moved)], out.at[pl.ds(0, moved)], sem).wait()
    pltpu.make_async_copy(tiles, tiles, sem).wait()
    row = lax.broadcasted_iota(jnp.int32, (16, LANES), 0)
    for shard in range(32):
        x = shard % 4
        if x:
            joined = jnp.where(row < (12 * x) % 16, real(tiles[1, shard - 1]), real(tiles[0, shard]))
            tiles[0, shard] = low(joined)
    for shard in range(32):
        pltpu.make_async_copy(tiles.at[0, shard], out.at[pl.ds(16 * ((403 * shard) // 4), 16)], sem).start()
    pltpu.make_async_copy(tiles.at[0], tiles.at[0], sem).wait()


def unpack(pos, pieces):
    hbm, vmem = pl.BlockSpec(memory_space=pl.ANY), pl.BlockSpec(memory_space=pltpu.VMEM)
    return pl.pallas_call(
        unpack_kernel,
        out_shape=jax.ShapeDtypeStruct((LINES, LANES), jnp.bfloat16),
        in_specs=[pl.BlockSpec(memory_space=pltpu.SMEM)] + [vmem] * 22,
        out_specs=hbm,
        scratch_shapes=[pltpu.VMEM((2, 32, 16, LANES), jnp.bfloat16), pltpu.SemaphoreType.DMA],
        compiler_params=pltpu.CompilerParams(vmem_limit_bytes=32 * 2**20),
        cost_estimate=pl.CostEstimate(flops=0, bytes_accessed=27_000_000, transcendentals=0),
        name="unpack_weights",
    )(pos, *pieces)


SPAN = 256
MICRO = 2
GROUPS = 8
ROWS = 256
F32 = jnp.float32


def nt(left, right, precision=None):
    return lax.dot_general(left, right, (((1,), (1,)), ((), ())), precision=precision, preferred_element_type=F32)


def tn(left, right, precision=None):
    return lax.dot_general(left, right, (((0,), (0,)), ((), ())), precision=precision, preferred_element_type=F32)


def nn(left, right, precision=None):
    return lax.dot_general(left, right, (((1,), (0,)), ((), ())), precision=precision, preferred_element_type=F32)


def sigmoid(v):
    return 0.5 + 0.5 * jnp.tanh(0.5 * v)


def iota(shape, dim):
    return lax.broadcasted_iota(jnp.int32, shape, dim)


def shifts(marks, first, length, step, offset):
    parts = []
    for d in range(1, 4):
        hit = iota((length, SPAN), 0) == iota((length, SPAN), 1) + step * d + offset
        parts.append(jnp.where(hit, marks[first + d - 1 : first + d, :], 0.0))
    return low(jnp.concatenate(parts, axis=1))


def by_head(ref, r):
    rows = [jnp.broadcast_to(ref[pl.ds(4 * r + k, 1), :], (HDIM, ref.shape[1])) for k in range(4)]
    return jnp.concatenate(rows, axis=0)


def put_head_sums(ref, r, block):
    for k in range(4):
        ref[pl.ds(4 * r + k, 1), :] = jnp.sum(block[k * HDIM : (k + 1) * HDIM], axis=0, keepdims=True)


def chunk(r):
    return pl.ds(pl.multiple_of(r * ROWS, ROWS), ROWS)


def prepare_kernel(
    ci, halo, taps, raw, steps, marks, conv, signal, inflow, maps, cum, step, cols, local, through, state, move, enter
):
    move[...] = shifts(marks, 0, SPAN, -1, 0)
    enter[...] = shifts(marks, 0, 16, -1, 3) * (iota((16, 3 * SPAN), 0) < 3).astype(jnp.bfloat16)
    step[...] = jax.nn.softplus(raw[...] + steps[:, 0:1])
    decay = -step[...] * steps[:, 1:2]
    upto = (iota((SPAN, SPAN), 0) <= iota((SPAN, SPAN), 1)).astype(F32)
    cum[...] = nn(decay, upto, lax.Precision.HIGHEST)
    column = lax.dot_general(
        upto, decay, (((0,), (1,)), ((), ())), precision=lax.Precision.HIGHEST, preferred_element_type=F32
    )
    for g in range(GROUPS):
        cols[g] = column[:, 4 * g : 4 * g + 4]
    ends = cum[:, SPAN - 1 : SPAN]
    state[...] = marks[7:8, :] * jnp.exp(ends - cum[...])
    through[0] = jnp.broadcast_to(marks[8:9, 0:1] * jnp.exp(ends), (HEADS, LANES))

    def convolve(r):
        x = ci[chunk(r), :]
        moved = nn(x, move[...]) + tn(halo[0, :, chunk(r)], enter[...])
        total = taps[chunk(r), 4:5] + real(x) * taps[chunk(r), 3:4]
        for d in range(1, 4):
            total = total + moved[:, (d - 1) * SPAN : d * SPAN] * taps[chunk(r), 3 - d : 4 - d]
        conv[chunk(r), :] = total
        return total * sigmoid(total)

    maps[...] = convolve(8)

    def channels(r, _):
        flow = convolve(r)
        signal[chunk(r), :] = flow
        x = flow * by_head(step, r)
        inflow[chunk(r), :] = low(x)
        tail = x * by_head(state, r)
        local[0, chunk(r), :] = low(nt(low(tail), low(maps[0:LANES, :])))
        return 0

    lax.fori_loop(0, 8, channels, 0)


def mixing(maps, docs, marks):
    products = tn(maps[0:LANES, :], maps[LANES:, :], lax.Precision.HIGHEST)
    inside = (docs[...] == marks[9:10, :]) & (iota((SPAN, SPAN), 0) <= iota((SPAN, SPAN), 1))
    return jnp.where(inside, products, 0.0)


def within_kernel(inflow, maps, cum, cols, docs, marks, out, table):
    @pl.when(pl.program_id(1) == 0)
    def _():
        table[...] = mixing(maps, docs, marks)

    half = SPAN // 2
    for h in range(4):
        row, col = cum[0, h : h + 1, :], cols[0, :, h : h + 1]
        upper = low(jnp.exp(jnp.minimum(row - col[:half], 0.0)) * table[:half, :])
        lower = low(jnp.exp(jnp.minimum(row[:, half:] - col[half:], 0.0)) * table[half:, half:])
        x = inflow[h * HDIM : (h + 1) * HDIM, :]
        y = nn(x[:, :half], upper)
        out[h * HDIM : (h + 1) * HDIM, :half] = y[:, :half]
        out[h * HDIM : (h + 1) * HDIM, half:] = y[:, half:] + nn(x[:, half:], lower)


def gate_kernel(
    inside, enter, maps, signal, gate, grad, cum, marks, coef,
    gated_low, grad_gate, grad_scan, carried_sum, skip_sum, gain_sum, grad_state, grad_read, scan, entry
):
    entry[...] = marks[6:7, :] * jnp.exp(cum[...])
    reads = low(maps[LANES:, :])

    @pl.when(pl.program_id(0) == 0)
    def _():
        gain_sum[...] = jnp.zeros_like(gain_sum)

    def forward(r, sums):
        carried = nn(enter[0, chunk(r), :], reads) * by_head(entry, r)
        total = inside[chunk(r), :] + carried + coef[chunk(r), 1:2] * signal[chunk(r), :]
        scan[chunk(r), :] = total
        z = gate[chunk(r), :]
        gated = total * (z * sigmoid(z))
        up = grad[chunk(r), :] * coef[chunk(r), 0:1]
        squares, cross = sums
        return (
            squares + jnp.sum(gated * gated, axis=0, keepdims=True),
            cross + jnp.sum(gated * up, axis=0, keepdims=True),
        )

    nothing = jnp.zeros((1, SPAN), F32)
    squares, cross = lax.fori_loop(0, 8, forward, (nothing, nothing))
    factor = lax.rsqrt(squares * (1.0 / DI) + EPSILON)
    pull = factor * factor * cross * (1.0 / DI)
    grad_read[...] = jnp.zeros_like(grad_read)

    def backward(r, _):
        heads = by_head(entry, r)
        state = enter[0, chunk(r), :]
        carried = nn(state, reads) * heads
        total = scan[chunk(r), :]
        z = gate[chunk(r), :]
        sig = sigmoid(z)
        soft = z * sig
        gated = total * soft
        scaled = gated * factor
        gain = coef[chunk(r), 0:1]
        given = grad[chunk(r), :]
        gated_low[chunk(r), :] = low(scaled * gain)
        share = given * scaled
        gain_sum[chunk(r), :] += share[:, :LANES] + share[:, LANES:]
        back = factor * (given * gain - gated * pull)
        grad_gate[chunk(r), :] = low(back * total * (sig * (1.0 + z * (1.0 - sig))))
        push = back * soft
        grad_scan[chunk(r), :] = push
        put_head_sums(carried_sum, r, push * carried)
        put_head_sums(skip_sum, r, push * signal[chunk(r), :])
        entering = low(push * heads)
        grad_state[0, chunk(r), :] = low(nt(entering, reads))
        grad_read[...] += tn(state, entering)
        return 0

    lax.fori_loop(0, 8, backward, 0)


def within_back_kernel(
    inflow, push, inside, maps, cum, cols, docs, marks, grad_inflow, decay_sum, grad_maps, table, grad_table
):
    g = pl.program_id(1)

    @pl.when(g == 0)
    def _():
        table[...] = mixing(maps, docs, marks)
        grad_table[...] = jnp.zeros_like(grad_table)

    half = SPAN // 2
    for h in range(4):
        rows = slice(h * HDIM, (h + 1) * HDIM)
        row, col = cum[0, h : h + 1, :], cols[0, :, h : h + 1]
        upper = jnp.exp(jnp.minimum(row - col[:half], 0.0))
        lower = jnp.exp(jnp.minimum(row[:, half:] - col[half:], 0.0))
        x, d = inflow[rows, :], low(push[rows, :])
        grad_table[:half, :] += upper * tn(x[:, :half], d)
        grad_table[half:, half:] += lower * tn(x[:, half:], d[:, half:])
        first = nt(d, low(upper * table[:half, :]))
        second = nt(d[:, half:], low(lower * table[half:, half:]))
        back = jnp.concatenate([first, second], axis=1)
        grad_inflow[rows, :] = back
        balance = real(d) * inside[rows, :] - real(x) * back
        decay_sum[0, h : h + 1, :] = jnp.sum(balance, axis=0, keepdims=True)

    @pl.when(g == GROUPS - 1)
    def _():
        inner = (docs[...] == marks[9:10, :]) & (iota((SPAN, SPAN), 0) <= iota((SPAN, SPAN), 1))
        spread = low(jnp.where(inner, grad_table[...], 0.0))
        grad_maps[0:LANES, :] = nt(low(maps[LANES:, :]), spread)
        grad_maps[LANES:, :] = nn(low(maps[0:LANES, :]), spread)


def state_back_kernel(
    leave, enter, conv, push, grad_inflow, maps, cum, step, raw, decay_sum, carried_sum, grad_maps, grad_read,
    steps, marks, coef, grad_conv, rim, grad_raw, bias_sum, rate_sum, tail, from_tail, from_step, crossing, grad_write
):
    ends = cum[:, SPAN - 1 : SPAN]
    tail[...] = marks[7:8, :] * jnp.exp(ends - cum[...])
    writes = low(maps[0:LANES, :])
    front = ((iota((16, SPAN), 1) == iota((16, SPAN), 0)) & (iota((16, SPAN), 0) < 3)).astype(jnp.bfloat16)
    grad_write[...] = grad_maps[0:LANES, :]

    def through_silu(r, c, sig, above):
        given = above * (sig * (1.0 + c * (1.0 - sig)))
        grad_conv[chunk(r), :] = given
        rim[0, :, chunk(r)] = low(nt(front, low(given)))

    def channels(r, _):
        c = conv[chunk(r), :]
        sig = sigmoid(c)
        signal = c * sig
        heads, tails = by_head(step, r), by_head(tail, r)
        x = signal * heads
        back = leave[0, chunk(r), :]
        ended = nn(back, writes) * tails
        whole = grad_inflow[chunk(r), :] + ended
        grad_write[...] += tn(back, low(x * tails))
        put_head_sums(from_tail, r, x * ended)
        put_head_sums(from_step, r, whole * signal)
        put_head_sums(crossing, r, real(back) * real(enter[0, chunk(r), :]))
        through_silu(r, c, sig, whole * heads + coef[chunk(r), 1:2] * push[chunk(r), :])
        return 0

    lax.fori_loop(0, 8, channels, 0)
    c = conv[chunk(8), :]
    through_silu(8, c, sigmoid(c), jnp.concatenate([grad_write[...], grad_maps[LANES:, :] + grad_read[...]], axis=0))
    last = iota((HEADS, SPAN), 1) == SPAN - 1
    passing = marks[8:9, 0:1] * jnp.exp(ends) * jnp.sum(crossing[...], axis=1, keepdims=True)
    tails = jnp.sum(from_tail[...], axis=1, keepdims=True)
    total = decay_sum[...] + carried_sum[...] - from_tail[...] + jnp.where(last, tails + passing, 0.0)
    onward = (iota((SPAN, SPAN), 0) >= iota((SPAN, SPAN), 1)).astype(F32)
    grad_decay = nn(total, onward, lax.Precision.HIGHEST)
    rate = steps[:, 1:2]
    rate_sum[...] = -grad_decay * step[...] * rate
    grad_step = (from_step[...] - grad_decay * rate) * sigmoid(raw[...] + steps[:, 0:1])
    bias_sum[...] = grad_step
    grad_raw[0:HEADS, :] = low(grad_step)
    grad_raw[HEADS:, :] = jnp.zeros((LANES - HEADS, SPAN), jnp.bfloat16)


def conv_back_kernel(grad_conv, ci, rim, taps, marks, grad_ci, sums, move, enter):
    @pl.when(pl.program_id(0) == 0)
    def _():
        for m in range(MICRO):
            here = marks[:, m * SPAN : (m + 1) * SPAN]
            move[m] = shifts(here, 3, SPAN, 1, 0)
            enter[m] = shifts(here, 3, 16, 1, -SPAN) * (iota((16, 3 * SPAN), 0) < 3).astype(jnp.bfloat16)

    totals = [0.0] * 5
    for m in range(MICRO):
        part = slice(m * SPAN, (m + 1) * SPAN)
        given, x = grad_conv[:, part], real(ci[:, part])
        moved = nn(low(given), move[m]) + tn(rim[m], enter[m])
        back = given * taps[:, 3:4]
        totals[3] += given * x
        totals[4] += given
        for d in range(1, 4):
            sooner = moved[:, (d - 1) * SPAN : d * SPAN]
            back += sooner * taps[:, 3 - d : 4 - d]
            totals[3 - d] += sooner * x
        grad_ci[:, part] = low(back)
    count = jnp.zeros((ROWS, LANES), F32)
    for k in range(5):
        pick = (iota((SPAN, LANES), 1) == k).astype(jnp.bfloat16)
        count += nn(low(totals[k]), pick)
    sums[...] = count[:, 0:8]


def call(kernel, grid, ins, outs, scratch, cost, name):
    return pl.pallas_call(
        kernel,
        grid=grid,
        in_specs=[pl.BlockSpec(block, where) for _, block, where in ins],
        out_specs=[pl.BlockSpec(block, where) for _, _, block, where in outs],
        out_shape=[jax.ShapeDtypeStruct(shape, dtype) for shape, dtype, _, _ in outs],
        scratch_shapes=scratch,
        compiler_params=pltpu.CompilerParams(
            vmem_limit_bytes=56 * 2**20, dimension_semantics=("arbitrary",) * len(grid)
        ),
        cost_estimate=pl.CostEstimate(flops=cost, bytes_accessed=20_000_000, transcendentals=0),
        name=name,
    )(*[array for array, _, _ in ins])


def neighbours(value, source, target):
    return lax.ppermute(value, GROUP, [(source, target)])


def chained(local, through, order, beside):
    keep = real(jnp.repeat(through[:, :, 0], HDIM, axis=1))[:, :, None]
    one = neighbours(local, order[0], order[1])
    two = neighbours(low(keep * real(one) + real(local)), order[1], order[2])
    two, beside = lax.optimization_barrier((two, beside))
    three = neighbours(low(keep * real(two) + real(local)), order[2], order[3])
    return one + two + three, beside


def shards(
    tokens, segments, cotangent, norm_gain, in_weight, conv_kernel, conv_bias, step_bias, decay_log,
    skip_gain, gate_gain, out_weight, master, moment_one, moment_two, step_count
):
    width = MICRO * SPAN
    bf16 = jnp.bfloat16
    spot = position()
    place = lax.axis_index(GROUP)
    ids = segments[:, 0, :]
    window = jnp.pad(ids, ((0, 0), (3, 3)), constant_values=-1)
    window = lax.dynamic_slice(window, (0, place * SPAN), (MICRO, SPAN + 6))
    here = window[:, 3 : 3 + SPAN]
    before = [window[:, 3 - d : 3 - d + SPAN] == here for d in (1, 2, 3)]
    after = [window[:, 3 + d : 3 + d + SPAN] == here for d in (1, 2, 3)]
    prior, final = window[:, 2:3], here[:, SPAN - 1 :]
    rows = before + after + [here == prior, here == final, jnp.broadcast_to(final == prior, here.shape)]
    marks = jnp.stack([row.astype(F32) for row in rows] + [here.astype(F32)] + [jnp.zeros(here.shape, F32)] * 6)
    marks = marks.reshape(16, width)
    docs = here.astype(F32).reshape(width, 1)

    norm_real = real(norm_gain)
    rows_in = real(tokens.reshape(width, D))
    normed, norm_back = jax.vjp(norm_piece, rows_in, norm_real)
    normed_low = low(normed)
    rim_tokens = lax.ppermute(tokens[:, 0, SPAN - 3 :, :], GROUP, [(0, 1), (1, 2), (2, 3)])
    rim_low = low(norm_piece(real(rim_tokens).reshape(-1, D), norm_real))
    rim_low = jnp.pad(rim_low.reshape(MICRO, 3, D), ((0, 0), (0, 13), (0, 0)))
    turned_weight = in_weight.T
    conv_weight = turned_weight[DI : DI + CH]
    halo = low(nt(rim_low.reshape(-1, D), conv_weight)).reshape(MICRO, 16, CH)
    ci = low(nt(conv_weight, normed_low))
    raw = nt(turned_weight[DI + CH :], normed_low)
    gate = nt(turned_weight[:DI], normed_low)
    upstream = cotangent.reshape(width, D)
    grad_mixed = nt(out_weight, upstream)

    taps = jnp.concatenate([real(conv_kernel), real(conv_bias)[None], jnp.zeros((3, CH), F32)]).T
    steps = jnp.stack([real(step_bias), jnp.exp(real(decay_log))] + [jnp.zeros((HEADS,), F32)] * 6, axis=1)
    coef = jnp.stack([real(gate_gain), jnp.repeat(real(skip_gain), HDIM)] + [jnp.zeros((DI,), F32)] * 6, axis=1)

    one, two = (MICRO,), (MICRO, GROUPS)
    by_m, by_gm = lambda m: (0, m), lambda m, g: (g, m)
    whole, first = lambda m: (0, 0), lambda m: (m, 0, 0)
    mark_in, mark_in2 = (marks, (16, SPAN), by_m), (marks, (16, SPAN), lambda m, g: (0, m))

    conv, signal, inflow, maps, cum, step, cols, local, through = call(
        prepare_kernel, one,
        [(ci, (CH, SPAN), by_m), (halo, (1, 16, CH), first), (taps, (CH, 8), whole), (raw, (HEADS, SPAN), by_m),
         (steps, (HEADS, 8), whole), mark_in],
        [((CH, width), F32, (CH, SPAN), by_m), ((DI, width), F32, (DI, SPAN), by_m),
         ((DI, width), bf16, (DI, SPAN), by_m), ((2 * STATE, width), F32, (2 * STATE, SPAN), by_m), ((HEADS, width), F32, (HEADS, SPAN), by_m),
         ((HEADS, width), F32, (HEADS, SPAN), by_m), ((GROUPS, width, 4), F32, (GROUPS, SPAN, 4), lambda m: (0, m, 0)),
         ((MICRO, DI, STATE), bf16, (1, DI, STATE), first), ((MICRO, HEADS, LANES), F32, (1, HEADS, LANES), first)],
        [pltpu.VMEM((HEADS, SPAN), F32), pltpu.VMEM((SPAN, 3 * SPAN), bf16), pltpu.VMEM((16, 3 * SPAN), bf16)],
        10**9, "convolve_and_prepare",
    )
    cum_groups = cum.reshape(GROUPS, 4, width)
    head_ins = [
        (maps, (2 * STATE, SPAN), lambda m, g: (0, m)),
        (cum_groups, (1, 4, SPAN), lambda m, g: (g, 0, m)),
        (cols, (1, SPAN, 4), lambda m, g: (g, m, 0)),
        (docs, (SPAN, 1), lambda m, g: (m, 0)),
        mark_in2,
    ]
    quad = (4 * HDIM, SPAN)
    table = pltpu.VMEM((SPAN, SPAN), F32)
    (inside,) = call(
        within_kernel, two, [(inflow, quad, by_gm)] + head_ins, [((DI, width), F32, quad, by_gm)], [table],
        4 * 10**9, "within_blocks",
    )

    enter, (inside, gate, grad_mixed) = chained(local, through, (0, 1, 2, 3), (inside, gate, grad_mixed))

    tall = (DI, SPAN)
    state_block = (1, DI, STATE)
    gated_low, grad_gate, push, carried_sum, skip_sum, gain_sum, grad_state, grad_read = call(
        gate_kernel, one,
        [(inside, tall, by_m), (enter, state_block, first), (maps, (2 * STATE, SPAN), by_m), (signal, tall, by_m),
         (gate, tall, by_m), (grad_mixed, tall, by_m), (cum, (HEADS, SPAN), by_m), mark_in, (coef, (DI, 8), whole)],
        [((DI, width), bf16, tall, by_m), ((DI, width), bf16, tall, by_m), ((DI, width), F32, tall, by_m),
         ((HEADS, width), F32, (HEADS, SPAN), by_m), ((HEADS, width), F32, (HEADS, SPAN), by_m),
         ((DI, LANES), F32, (DI, LANES), whole), ((MICRO, DI, STATE), bf16, state_block, first),
         ((STATE, width), F32, (STATE, SPAN), by_m)],
        [pltpu.VMEM((DI, SPAN), F32), pltpu.VMEM((HEADS, SPAN), F32)], 2 * 10**9, "gate_and_back",
    )
    grad_inflow, decay_sum, grad_maps = call(
        within_back_kernel, two,
        [(inflow, quad, by_gm), (push, quad, by_gm), (inside, quad, by_gm)] + head_ins,
        [((DI, width), F32, quad, by_gm), ((GROUPS, 4, width), F32, (1, 4, SPAN), lambda m, g: (g, 0, m)),
         ((2 * STATE, width), F32, (2 * STATE, SPAN), lambda m, g: (0, m))],
        [table, table], 8 * 10**9, "within_blocks_back",
    )

    leave, (grad_inflow, decay_sum, grad_maps) = chained(
        grad_state, through, (3, 2, 1, 0), (grad_inflow, decay_sum, grad_maps)
    )

    few = (HEADS, SPAN)
    grad_conv, rim, grad_raw, bias_sum, rate_sum = call(
        state_back_kernel, one,
        [(leave, state_block, first), (enter, state_block, first), (conv, (CH, SPAN), by_m), (push, tall, by_m),
         (grad_inflow, tall, by_m), (maps, (2 * STATE, SPAN), by_m), (cum, few, by_m), (step, few, by_m), (raw, few, by_m),
         (decay_sum.reshape(HEADS, width), few, by_m), (carried_sum, few, by_m), (grad_maps, (2 * STATE, SPAN), by_m),
         (grad_read, (STATE, SPAN), by_m), (steps, (HEADS, 8), whole), mark_in, (coef, (DI, 8), whole)],
        [((CH, width), F32, (CH, SPAN), by_m), ((MICRO, 16, CH), bf16, (1, 16, CH), first),
         ((LANES, width), bf16, (LANES, SPAN), by_m), ((HEADS, width), F32, few, by_m), ((HEADS, width), F32, few, by_m)],
        [pltpu.VMEM(few, F32), pltpu.VMEM(few, F32), pltpu.VMEM(few, F32), pltpu.VMEM((HEADS, LANES), F32),
         pltpu.VMEM((STATE, SPAN), F32)], 10**9, "state_and_silu_back",
    )
    next_rim = lax.ppermute(rim, GROUP, [(1, 0), (2, 1), (3, 2)])

    by_r = lambda r: (r, 0)
    grad_ci, tap_sums = call(
        conv_back_kernel, (CH // ROWS,),
        [(grad_conv, (ROWS, width), by_r), (ci, (ROWS, width), by_r), (next_rim, (MICRO, 16, ROWS), lambda r: (0, 0, r)),
         (taps, (ROWS, 8), by_r), (marks, (16, width), lambda r: (0, 0))],
        [((CH, width), bf16, (ROWS, width), by_r), ((CH, 8), F32, (ROWS, 8), by_r)],
        [pltpu.VMEM((MICRO, SPAN, 3 * SPAN), bf16), pltpu.VMEM((MICRO, 16, 3 * SPAN), bf16)], 10**8, "convolution_back",
    )

    grad_normed = (
        tn(grad_gate, turned_weight[:DI]) + tn(grad_ci, conv_weight) + tn(grad_raw[:HEADS], turned_weight[DI + CH :])
    )
    grad_rows, grad_norm_gain = norm_back(grad_normed)
    input_grad = low(real(upstream) + grad_rows).reshape(tokens.shape)
    output = low(rows_in + tn(gated_low, out_weight)).reshape(tokens.shape)

    left = normed_low.T.reshape(D // 4, 4, width).transpose(1, 0, 2).reshape(D, width)
    turned = jnp.concatenate([upstream[:, 32:], upstream[:, :32]], axis=1)
    middle = [tap_sums[:, :5].T.reshape(-1), jnp.sum(bias_sum, axis=1), jnp.sum(rate_sum, axis=1)]
    middle += [jnp.sum(skip_sum, axis=1), jnp.sum(gain_sum, axis=1), jnp.zeros((32 + 5 * LANES,), F32)]
    middle = jnp.concatenate(middle).reshape(-1, LANES)
    packed = pack(spot, left, grad_gate, grad_ci, grad_raw, gated_low, turned, grad_norm_gain.reshape(-1, LANES), middle)
    piece = reduce_pieces(packed[:3], packed[3:])
    window = lax.all_gather(piece, GROUP, axis=0, tiled=True)
    skew = (12 * lax.axis_index("x")) % 16
    shard = lax.dynamic_slice(window, (skew, 0), (SHARD_LINES, LANES)).reshape(-1)
    squares = over_copies(jnp.sum(shard * shard), DP)
    clip_factor = MAX_NORM / jnp.maximum(jnp.sqrt(squares), MAX_NORM)
    first_moment, second_moment, updated = adam_update(
        shard * clip_factor, master, moment_one, moment_two, step_count
    )
    blank = jnp.zeros_like(window)
    placed = low(lax.dynamic_update_slice(blank, updated.reshape(SHARD_LINES, LANES), (skew, 0)))
    mine = lax.dynamic_slice(placed, (PIECE * place, 0), (PIECE, LANES))
    copies = unpack(spot, gather_pieces(mine)).reshape(-1)
    return (output, input_grad, shard, first_moment, second_moment, updated, copies)


def solution(mesh):
    finer = Mesh(mesh.devices.reshape(4, 2, 4, 2, 2), ("y", "zl", "x", "zh", "core"))
    return jax.shard_map(
        shards,
        mesh=finer,
        in_specs=(
            P(None, DP, GROUP, None),
            P(None, DP, None),
            P(None, DP, GROUP, None),
            P(),
            P(),
            P(),
            P(),
            P(),
            P(),
            P(),
            P(),
            P(),
            P(DP),
            P(DP),
            P(DP),
            P(),
        ),
        out_specs=(
            P(None, DP, GROUP, None),
            P(None, DP, GROUP, None),
            P(DP),
            P(DP),
            P(DP),
            P(DP),
            P(),
        ),
        check_vma=False,
    )
```

time: 836 us -> 456 us (0.55)
  other arithmetic: 203 us -> 39.3 us
  matrix products: 153 us -> 45.6 us
  local copies, waits for them, and re-layouts: 132 us -> 34.2 us
  Pallas kernels: 81.9 us -> 130 us
  waiting for transfers between devices: 105 us -> 84.4 us
  between operations: 20.7 us -> 3.28 us
  blocking collectives: 27.7 us -> 14.3 us
    dot_general x32 -> x9, matrix products: 153 us -> 45.6 us  [the longest x5 25.8 us: nt(): lax.dot_general(left, right, (((1,), (1,)), ((), ())), precision=precisio...]
    pallas_call x0 -> x6, Pallas kernels: none -> 90.8 us  [call(): pl.pallas_call(kernel, grid=grid, in_specs=[pl.BlockSpec(block, where) fo...]
    reduce_sum x16 -> x7, other arithmetic: 46.5 us -> 2.25 us  [the longest x3 1.56 us: exchange_sum(): return jnp.sum(real(exchange(block, axis)), axis=0)]
    pallas_call x1, Pallas kernels: 65.2 us -> 24.5 us  [pack(): pl.pallas_call(pack_kernel, out_shape=shapes + shapes, in_specs=[pl.Block...]
    select_n x12 -> x0, other arithmetic: 31.3 us -> none  [step(): jnp.where(position < mine, new, old)]
    all_to_all x0 -> x6, waiting for transfers between devices: none -> 28.9 us  [exchange(): lax.all_to_all(blocks, RING[axis], split_axis=0, concat_axis=0, tiled=True)]
    ppermute x21 -> x14, waiting for transfers between devices: 47.1 us -> 18.6 us  [from_offset(): return lax.ppermute(block, RING[axis], route)]
    ppermute x21 -> x14, waiting for transfers between devices: 45.2 us -> 20 us  [to_offset(): return lax.ppermute(block, RING[axis], route)]
  transfers between devices with their start and end apart: 66 -> 57, of which waited for: 24 -> 25; matrix products, arithmetic and copies ran while one was open for 27% -> 17% of each run, Pallas kernels for 0% -> 7%
where the time goes in v2:
time: 456 us; the launch traced here: 451 us
  Pallas kernels  130 us (29%)
  starting transfers between devices  99.7 us (22%)
  waiting for transfers between devices  84.4 us (19%)
  matrix products  45.6 us (10%)
  other arithmetic  39.3 us (9%)
  local copies, waits for them, and re-layouts  34.2 us (8%)
  blocking collectives  14.3 us (3%)
    pallas_call x6, Pallas kernels, call(): pl.pallas_call(kernel, grid=grid, in_specs=[pl.BlockSpec(block, where) fo...  90.8 us
    all_to_all x6, waiting for transfers between devices, exchange(): lax.all_to_all(blocks, RING[axis], split_axis=0, concat_axis=0, tiled=True)  28.9 us
    dot_general x5, matrix products, nt(): lax.dot_general(left, right, (((1,), (1,)), ((), ())), precision=precisio...  25.8 us
    pallas_call x1, Pallas kernels, pack(): pl.pallas_call(pack_kernel, out_shape=shapes + shapes, in_specs=[pl.Block...  24.5 us
    ppermute x6, starting transfers between devices, neighbours(): return lax.ppermute(value, GROUP, [(source, target)])  21.9 us
    convert_element_type x15, other arithmetic, low(): return v.astype(jnp.bfloat16)  21.5 us
    all_to_all x6, starting transfers between devices, exchange(): lax.all_to_all(blocks, RING[axis], split_axis=0, concat_axis=0, tiled=True)  21.4 us
    ppermute x14, waiting for transfers between devices, to_offset(): return lax.ppermute(block, RING[axis], route)  20 us
  transfers between devices with their start and end apart: 57, of which 25 were waited for; matrix products, arithmetic and copies ran while one was open for 17% of the time, Pallas kernels for 7%

profile of v2, /device:TPU:1, one launch (start us, length us, event | category | flops | bytes accessed | tf_op | source)
XLA Modules:
  0.0 451.1 jit_solution(14297279151215443312)
XLA Ops:
  1.4 6.9 %collective-permute-start = (bf16[2,3,1024]{2,1,0:T(4,128)(2,1)S(1)}, bf16[2,3,1024]{2,1,0:T(4,128)(2,1)S(1)}, u32[]{:S(2)}, u32[]{:S(2)}) collective-permute-start(bf16[2,3,1024]{2,1,0:T(4,128)(2,1)S(1)} %slice_bitcast_fusion.13), channel_id=1, source_target_pairs={{0,1},{1,2},{2,3},{4,5},{5,6},{6,7},{8,9},{9,10},{10,11},{12,13},{... | collective-permute-start | bytes 36872 | tf_op jit(solution)/shard_map/ppermute | solution.py:727
  13.2 6.3 %fusion.ci = bf16[2304,512]{1,0:T(8,128)(2,1)} fusion(bf16[512,1024]{1,0:T(8,128)(2,1)S(1)} %fusion.24, bf16[4384,1024]{1,0:T(8,128)(2,1)} %bitcast.239), kind=kOutput, calls=%fused_computation.4 | convolution fusion | flops 2417098752 | bytes 8126464 | tf_op jit(solution)/shard_map/dot_general | solution.py:401
  25.9 4.5 fusion.10
  30.4 16.3 %convolve_and_prepare.1 = (f32[2304,512]{1,0:T(8,128)}, f32[2048,512]{1,0:T(8,128)}, bf16[2048,512]{1,0:T(8,128)(2,1)}, f32[256,512]{1,0:T(8,128)}, f32[32,512]{...) custom-call(bf16[2304,512]{1,0:T(8,128)(2,1)} %fusion.ci, ...), custom_call_target="tpu_custom_call" | custom-call | flops 1000000000 | bytes 20000000 | tf_op jit(solution)/shard_map/convolve_and_prepare/pallas_call | solution.py:675
  56.4 6.6 %fusion.13.gate = f32[2048,512]{1,0:T(8,128)} fusion(bf16[512,1024]{1,0:T(8,128)(2,1)S(1)} %fusion.24, bf16[4384,1024]{1,0:T(8,128)(2,1)} %bitcast.242), kind=kOutput, calls=%fused_computation.15 | convolution fusion | flops 2147483648 | bytes 9437184 | tf_op jit(solution)/shard_map/dot_general | solution.py:401
  63.9 6.6 %fusion.71.grad = f32[2048,512]{1,0:T(8,128)} fusion(bf16[2048,1024]{1,0:T(8,128)(2,1)} %param.27, bf16[512,1024]{1,0:T(8,128)(2,1)S(1)} %bitcast.200), kind=kOutput, calls=%fused_computation.172 | convolution fusion | flops 2147483648 | bytes 9437184 | tf_op jit(solution)/shard_map/dot_general | solution.py:401
  71.1 14.1 %within_blocks.1.inside = f32[2048,512]{1,0:T(8,128)} custom-call(bf16[2048,512]{1,0:T(8,128)(2,1)} %get-tuple-element.50.inflow, f32[256,512]{1,0:T(8,128)} %get-tuple-element.51.maps, f32[8,4,512]{2,1,0:T(4,128)} %reshape.226.cum, f32[8,512,4]{2,1,0:T(8,128)} %get-tuple-element.53.cols, f32[512,1]{1,0:T(8,128)} %bitcast.219, f32[16,512]{1,0:T(8,128)} %stack.132.marks), custom_call_target="tpu_custom_call" | custom-call | flops 4000000000 | bytes 20000000 | tf_op jit(solution)/shard_map/within_blocks/pallas_call | solution.py:675
  87.8 13.9 %collective-permute-start.3 = (bf16[2,2048,128]{2,1,0:T(8,128)(2,1)}, bf16[2,2048,128]{2,1,0:T(8,128)(2,1)}, u32[]{:S(2)}, u32[]{:S(2)}) collective-permute-start(bf16[2,2048,128]{2,1,0:T(8,128)(2,1)} %fusion.17), channel_id=1, source_target_pairs={{2,3},{6,7},{10,11},{14,15},{18,19},{22,23},{26,27},{30,31},{34,35... | collective-permute-start | bytes 3145736 | tf_op jit(solution)/shard_map/ppermute | solution.py:691
  105.9 19.1 %gate_and_back.1 = (bf16[2048,512]{1,0:T(8,128)(2,1)}, bf16[2048,512]{1,0:T(8,128)(2,1)}, f32[2048,512]{1,0:T(8,128)}, f32[32,512]{1,0:T(8,128)}, f32[32,512]{1,...) custom-call(f32[2048,512]{1,0:T(8,128)} %within_blocks.1.inside, ...), custom_call_target="tpu_custom_call" | custom-call | flops 2000000000 | bytes 20000000 | tf_op jit(solution)/shard_map/gate_and_back/pallas_call | solution.py:675
  128.8 17.0 %within_blocks_back.1 = (f32[2048,512]{1,0:T(8,128)}, f32[8,4,512]{2,1,0:T(4,128)}, f32[256,512]{1,0:T(8,128)}) custom-call(bf16[2048,512]{1,0:T(8,128)(2,1)} %get-tuple-element.50.inflow, f32[2048,512]{1,0:T(8,128)} %get-tuple-element.62.push, f32[2048,512]{1,0:T(8,128)} %within_blocks.1.inside, f32[256,512]{1,0:T(8,128)} %get-tuple-element.51.maps, ...), custom_call_target="tpu_custom_call" | custom-call | flops 8000000000 | bytes 20000000 | tf_op jit(solution)/shard_map/within_blocks_back/pallas_call | solution.py:675
  162.2 12.4 %state_and_silu_back.1 = (f32[2304,512]{1,0:T(8,128)}, bf16[2,16,2304]{2,1,0:T(8,128)(2,1)}, bf16[128,512]{1,0:T(8,128)(2,1)}, f32[32,512]{1,0:T(8,128)}, f32[32,512]{1,0:T(8,128)}) custom-call(bf16[2,2048,128]{2,1,0:T(8,128)(2,1)} %add_add_fusion.2.leave, bf16[2,2048,128]{2,1,0:T(8,128)(2,1)} %add_add_fusion.3.enter, f32[2304,512]{1,0:T(8,128)} %get-tuple-element.67.conv, ...), custom_call_target="tpu_custom_call" | custom-call | flops 1000000000 | bytes 20000000 | tf_op jit(solution)/shard_map/state_and_silu_back/pallas_call | solution.py:675
  176.6 4.6 %fusion.1 = f32[512,1024]{1,0:T(8,128)S(1)} fusion(bf16[2048,512]{1,0:T(8,128)(2,1)S(1)} %copy-done.29, bf16[4384,1024]{1,0:T(8,128)(2,1)} %bitcast.243), kind=kOutput, calls=%fused_computation.5 | convolution fusion | flops 2147483648 | bytes 8388608 | tf_op jit(solution)/shard_map/dot_general | solution.py:405
  183.6 11.9 %convolution_back.1 = (bf16[2304,512]{1,0:T(8,128)(2,1)}, f32[2304,8]{1,0:T(8,128)}) custom-call(f32[2304,512]{1,0:T(8,128)} %get-tuple-element.74.grad_conv, bf16[2304,512]{1,0:T(8,128)(2,1)} %fusion.ci, bf16[2,16,2304]{2,1,0:T(8,128)(2,1)} %copy-done.20, f32[2304,8]{1,0:T(8,128)} %bitcast.194, f32[16,512]{1,0:T(8,128)} %stack.132.marks), custom_call_target="tpu_custom_call" | custom-call | flops 100000000 | bytes 20000000 | tf_op jit(solution)/shard_map/convolution_back/pallas_call | solution.py:675
  197.2 5.3 %fusion.5 = f32[512,1024]{1,0:T(8,128)S(1)} fusion(bf16[2304,512]{1,0:T(8,128)(2,1)} %get-tuple-element.76.grad_ci, bf16[4384,1024]{1,0:T(8,128)(2,1)} %bitcast.244), kind=kOutput, calls=%fused_computation.9 | convolution fusion | flops 2415919104 | bytes 9175040 | tf_op jit(solution)/shard_map/dot_general | solution.py:405
  202.5 3.7 fusion.25
  206.9 24.5 %pack_gradients.1 = (bf16[9216,128]{1,0:T(8,128)(2,1)}, bf16[9216,128]{1,0:T(8,128)(2,1)}, bf16[8192,128]{1,0:T(8,128)(2,1)}, bf16[9216,128]{1,0:T(8,128)(2,1)},...) custom-call(s32[4]{0:T(128)} %pad_add_fusion.pos, bf16[1024,512]{1,0:T(8,128)(2,1)} %bitcast.212, ...), custom_call_target="tpu_custom_call" | custom-call | flops 7000000000 | bytes 25000000 | tf_op jit(solution)/shard_map/pack_gradients/pallas_call | solution.py:192
  232.1 5.8 %collective-permute-done.18 = bf16[8192,128]{1,0:T(8,128)(2,1)S(1)} collective-permute-done((bf16[8192,128]{1,0:T(8,128)(2,1)}, bf16[8192,128]{1,0:T(8,128)(2,1)S(1)}, u32[]{:S(2)}, u32[]{:S(2)}) %collective-permute-start.18) | collective-permute-done | bytes 2097184 | tf_op jit(solution)/shard_map/ppermute | solution.py:83
  241.4 3.9 all-to-all-start.1
  265.9 8.5 %collective-permute-done.10 = bf16[2304,128]{1,0:T(8,128)(2,1)S(1)} collective-permute-done((bf16[2304,128]{1,0:T(8,128)(2,1)S(1)}, bf16[2304,128]{1,0:T(8,128)(2,1)S(1)}, u32[]{:S(2)}, u32[]{:S(2)}) %collective-permute-start.10) | collective-permute-done | bytes 589856 | tf_op jit(solution)/shard_map/ppermute | solution.py:220
  278.4 3.6 all-to-all-start
  293.7 4.0 all-to-all-done
  306.9 4.6 %all-to-all-done.2 = bf16[4,144,128]{2,1,0:T(8,128)(2,1)S(1)} async-done(((bf16[4,144,128]{2,1,0:T(8,128)(2,1)}), bf16[4,144,128]{2,1,0:T(8,128)(2,1)S(1)}, u32[]{:S(2)}, u32[]{:S(2)}) %all-to-all-start.2) | async-done | bytes 147488 | tf_op jit(solution)/shard_map/all_to_all | solution.py:225
  311.5 14.3 %all_gather.3 = f32[1664,128]{1,0:T(8,128)S(1)} all-gather(f32[416,128]{1,0:T(8,128)S(1)} %pad_maximum_fusion.6), channel_id=1, replica_groups=mesh['y'=4,'zl'=2,'x'=4,'zh'=2,'core'=2] {'zh','core'}, dimensions={0}, use_global_device_ids=true | all-gather | bytes 1064960 | tf_op jit(solution)/shard_map/all_gather | solution.py:837
  327.9 3.8 all-to-all-start.3
  331.8 7.1 %all-to-all-done.3 = f32[32,1,1]{2,1,0:T(1,128)S(1)} async-done(((f32[32,1,1]{2,1,0:T(1,128)}), f32[32,1,1]{2,1,0:T(1,128)S(1)}, u32[]{:S(2)}, u32[]{:S(2)}) %all-to-all-start.3) | async-done | bytes 160 | tf_op jit(solution)/shard_map/all_to_all | solution.py:32
  350.8 4.5 %all-to-all-done.4 = bf16[4,144,128]{2,1,0:T(8,128)(2,1)S(1)} async-done(((bf16[4,144,128]{2,1,0:T(8,128)(2,1)}), bf16[4,144,128]{2,1,0:T(8,128)(2,1)S(1)}, u32[]{:S(2)}, u32[]{:S(2)}) %all-to-all-start.4) | async-done | bytes 147488 | tf_op jit(solution)/shard_map/all_to_all | solution.py:225
  368.1 8.0 %all-to-all-done.5 = bf16[4,1152,128]{2,1,0:T(8,128)(2,1)S(1)} async-done(((bf16[4,1152,128]{2,1,0:T(8,128)(2,1)}), bf16[4,1152,128]{2,1,0:T(8,128)(2,1)S(1)}, u32[]{:S(2)}, u32[]{:S(2)}) %all-to-all-start.5) | async-done | bytes 1179680 | tf_op jit(solution)/shard_map/all_to_all | solution.py:225
  377.8 3.6 all-to-all-start.6
  390.5 7.4 %collective-permute-done.28.rest_1_ = bf16[2304,128]{1,0:T(8,128)(2,1)S(1)} collective-permute-done((bf16[2304,128]{1,0:T(8,128)(2,1)S(1)}, bf16[2304,128]{1,0:T(8,128)(2,1)S(1)}, u32[]{:S(2)}, u32[]{:S(2)}) %collective-permute-start.28) | collective-permute-done | bytes 589856 | tf_op jit(solution)/shard_map/ppermute | solution.py:79
  399.8 7.7 %all-to-all-done.6 = bf16[4,2048,128]{2,1,0:T(8,128)(2,1)S(1)} async-done(((bf16[4,2048,128]{2,1,0:T(8,128)(2,1)}), bf16[4,2048,128]{2,1,0:T(8,128)(2,1)S(1)}, u32[]{:S(2)}, u32[]{:S(2)}) %all-to-all-start.6) | async-done | bytes 2097184 | tf_op jit(solution)/shard_map/all_to_all | solution.py:225
  427.9 6.1 %fusion.27 = bf16[512,1024]{1,0:T(8,128)(2,1)} fusion(bf16[2,1,256,1024]{3,2,1,0:T(8,128)(2,1)S(1)} %copy-done.4, bf16[2048,512]{1,0:T(8,128)(2,1)} %get-tuple-element.59.gated, bf16[2048,1024]{1,0:T(8,128)(2,1)} %param.27), kind=kOutput, calls=%fused_computation.37 | convolution fusion | flops 2149056512 | bytes 8388608 | tf_op jit(solution)/shard_map/dot_general | solution.py:405
  435.7 15.1 %unpack_weights.1 = bf16[51584,128]{1,0:T(8,128)(2,1)} custom-call(s32[4]{0:T(128)S(1)} %copy-done.2, bf16[2304,128]{1,0:T(8,128)(2,1)S(1)} %bitcast.191, bf16[2304,128]{1,0:T(8,128)(2,1)S(1)} %copy-done.1, bf16[2304,128]{1,0:T(8,128)(2,1)} %collective-permute-done.29.rest_2_, bf16[1152,128]{1,0:T(8,128)(2,1)S(1)} %collective-permute-done.30.rest_3_, ...), custom_call_target="tpu_custom_call" | custom-call | bytes 27000000 | tf_op jit(solution)/shard_map/unpack_weights/pallas_call | solution.py:381
  (298 shorter events, 165.8 us)
Async XLA Ops:
  1.4 24.3 %collective-permute-start = (bf16[2,3,1024]{2,1,0:T(4,128)(2,1)S(1)}, bf16[2,3,1024]{2,1,0:T(4,128)(2,1)S(1)}, u32[]{:S(2)}, u32[]{:S(2)}) collective-permute-start(bf16[2,3,1024]{2,1,0:T(4,128)(2,1)S(1)} %slice_bitcast_fusion.13), channel_id=1, source_target_pairs={{0,1},{1,2},{2,3},{4,5},{5,6},{6,7},{8,9},{9,10},{10,11},{12,13},{... | collective-permute-start | bytes 36872 | tf_op jit(solution)/shard_map/ppermute | solution.py:727
  54.0 31.2 %collective-permute-start.2 = (bf16[2,2048,128]{2,1,0:T(8,128)(2,1)}, bf16[2,2048,128]{2,1,0:T(8,128)(2,1)}, u32[]{:S(2)}, u32[]{:S(2)}) collective-permute-start(bf16[2,2048,128]{2,1,0:T(8,128)(2,1)} %fusion.16), channel_id=1, source_target_pairs={{1,2},{5,6},{9,10},{13,14},{17,18},{21,22},{25,26},{29,30},{33,34}... | collective-permute-start | bytes 3145736 | tf_op jit(solution)/shard_map/ppermute | solution.py:691
  87.8 15.5 %collective-permute-start.3 = (bf16[2,2048,128]{2,1,0:T(8,128)(2,1)}, bf16[2,2048,128]{2,1,0:T(8,128)(2,1)}, u32[]{:S(2)}, u32[]{:S(2)}) collective-permute-start(bf16[2,2048,128]{2,1,0:T(8,128)(2,1)} %fusion.17), channel_id=1, source_target_pairs={{2,3},{6,7},{10,11},{14,15},{18,19},{22,23},{26,27},{30,31},{34,35... | collective-permute-start | bytes 3145736 | tf_op jit(solution)/shard_map/ppermute | solution.py:691
  127.5 18.3 %collective-permute-start.5 = (bf16[2,2048,128]{2,1,0:T(8,128)(2,1)S(1)}, bf16[2,2048,128]{2,1,0:T(8,128)(2,1)S(1)}, u32[]{:S(2)}, u32[]{:S(2)}) collective-permute-start(bf16[2,2048,128]{2,1,0:T(8,128)(2,1)S(1)} %fusion.18), channel_id=1, source_target_pairs={{2,1},{6,5},{10,9},{14,13},{18,17},{22,21},{26,25},{30,29},{34,33}... | collective-permute-start | bytes 3145736 | tf_op jit(solution)/shard_map/ppermute | solution.py:691
  147.4 12.5 %collective-permute-start.6 = (bf16[2,2048,128]{2,1,0:T(8,128)(2,1)}, bf16[2,2048,128]{2,1,0:T(8,128)(2,1)}, u32[]{:S(2)}, u32[]{:S(2)}) collective-permute-start(bf16[2,2048,128]{2,1,0:T(8,128)(2,1)} %fusion.19), channel_id=1, source_target_pairs={{1,0},{5,4},{9,8},{13,12},{17,16},{21,20},{25,24},{29,28},{33,32},... | collective-permute-start | bytes 3145736 | tf_op jit(solution)/shard_map/ppermute | solution.py:691
  231.5 13.8 %collective-permute-start.8 = (bf16[9216,128]{1,0:T(8,128)(2,1)}, bf16[9216,128]{1,0:T(8,128)(2,1)}, u32[]{:S(2)}, u32[]{:S(2)}) collective-permute-start(bf16[9216,128]{1,0:T(8,128)(2,1)} %get-tuple-element.84), channel_id=1, source_target_pairs={{0,1},{1,0},{2,3},{3,2},{4,5},{5,4},{6,7},{7,6},{8,9},{9,8},{10,11... | collective-permute-start | bytes 7077896 | tf_op jit(solution)/shard_map/ppermute | solution.py:83
  232.0 18.7 %collective-permute-start.13 = (bf16[9216,128]{1,0:T(8,128)(2,1)}, bf16[9216,128]{1,0:T(8,128)(2,1)}, u32[]{:S(2)}, u32[]{:S(2)}) collective-permute-start(bf16[9216,128]{1,0:T(8,128)(2,1)} %get-tuple-element.86), channel_id=1, source_target_pairs={{0,1},{1,0},{2,3},{3,2},{4,5},{5,4},{6,7},{7,6},{8,9},{9,8},{10,11... | collective-permute-start | bytes 7077896 | tf_op jit(solution)/shard_map/ppermute | solution.py:83
  241.4 37.1 %all-to-all-start.1 = ((bf16[4,2048,128]{2,1,0:T(8,128)(2,1)}), bf16[4,2048,128]{2,1,0:T(8,128)(2,1)S(1)}, u32[]{:S(2)}, u32[]{:S(2)}) async-start(bf16[4,2048,128]{2,1,0:T(8,128)(2,1)} %bitcast.44), calls=%async_computation.1 | async-start | bytes 4194304 | tf_op jit(solution)/shard_map/all_to_all | solution.py:225
  250.7 9.0 %collective-permute-start.9 = (bf16[1152,128]{1,0:T(8,128)(2,1)S(1)}, bf16[1152,128]{1,0:T(8,128)(2,1)S(1)}, u32[]{:S(2)}, u32[]{:S(2)}) collective-permute-start(bf16[1152,128]{1,0:T(8,128)(2,1)S(1)} %get-tuple-element.134), channel_id=1, source_target_pairs={{0,4},{4,8},{8,12},{12,0},{1,5},{5,9},{9,13},{13,1},{2,6},{6,10},{... | collective-permute-start | bytes 884744 | tf_op jit(solution)/shard_map/ppermute | solution.py:220
  252.7 10.0 %collective-permute-start.14 = (bf16[1152,128]{1,0:T(8,128)(2,1)S(1)}, bf16[1152,128]{1,0:T(8,128)(2,1)S(1)}, u32[]{:S(2)}, u32[]{:S(2)}) collective-permute-start(bf16[1152,128]{1,0:T(8,128)(2,1)S(1)} %get-tuple-element.140), channel_id=1, source_target_pairs={{0,32},{32,64},{64,96},{96,0},{1,33},{33,65},{65,97},{97,1},{2,34}... | collective-permute-start | bytes 884744 | tf_op jit(solution)/shard_map/ppermute | solution.py:220
  254.1 8.7 %collective-permute-start.16 = (bf16[1152,128]{1,0:T(8,128)(2,1)S(1)}, bf16[1152,128]{1,0:T(8,128)(2,1)S(1)}, u32[]{:S(2)}, u32[]{:S(2)}) collective-permute-start(bf16[1152,128]{1,0:T(8,128)(2,1)S(1)} %get-tuple-element.141), channel_id=1, source_target_pairs={{0,96},{32,0},{64,32},{96,64},{1,97},{33,1},{65,33},{97,65},{2,98}... | collective-permute-start | bytes 884744 | tf_op jit(solution)/shard_map/ppermute | solution.py:220
  259.9 14.5 %collective-permute-start.10 = (bf16[2304,128]{1,0:T(8,128)(2,1)S(1)}, bf16[2304,128]{1,0:T(8,128)(2,1)S(1)}, u32[]{:S(2)}, u32[]{:S(2)}) collective-permute-start(bf16[2304,128]{1,0:T(8,128)(2,1)S(1)} %pad_maximum_fusion.2), channel_id=1, source_target_pairs={{0,4},{4,8},{8,12},{12,0},{1,5},{5,9},{9,13},{13,1},{2,6},{6,10},{... | collective-permute-start | bytes 1769480 | tf_op jit(solution)/shard_map/ppermute | solution.py:220
  260.1 14.4 %collective-permute-start.12 = (bf16[2304,128]{1,0:T(8,128)(2,1)S(1)}, bf16[2304,128]{1,0:T(8,128)(2,1)S(1)}, u32[]{:S(2)}, u32[]{:S(2)}) collective-permute-start(bf16[2304,128]{1,0:T(8,128)(2,1)S(1)} %pad_maximum_fusion.3), channel_id=1, source_target_pairs={{0,12},{4,0},{8,4},{12,8},{1,13},{5,1},{9,5},{13,9},{2,14},{6,2},{... | collective-permute-start | bytes 1769480 | tf_op jit(solution)/shard_map/ppermute | solution.py:220
  263.0 14.1 %collective-permute-start.15 = (bf16[2304,128]{1,0:T(8,128)(2,1)S(1)}, bf16[2304,128]{1,0:T(8,128)(2,1)S(1)}, u32[]{:S(2)}, u32[]{:S(2)}) collective-permute-start(bf16[2304,128]{1,0:T(8,128)(2,1)S(1)} %pad_maximum_fusion.4), channel_id=1, source_target_pairs={{0,32},{32,64},{64,96},{96,0},{1,33},{33,65},{65,97},{97,1},{2,34}... | collective-permute-start | bytes 1769480 | tf_op jit(solution)/shard_map/ppermute | solution.py:220
  264.4 12.7 %collective-permute-start.17 = (bf16[2304,128]{1,0:T(8,128)(2,1)S(1)}, bf16[2304,128]{1,0:T(8,128)(2,1)S(1)}, u32[]{:S(2)}, u32[]{:S(2)}) collective-permute-start(bf16[2304,128]{1,0:T(8,128)(2,1)S(1)} %pad_maximum_fusion.5), channel_id=1, source_target_pairs={{0,96},{32,0},{64,32},{96,64},{1,97},{33,1},{65,33},{97,65},{2,98}... | collective-permute-start | bytes 1769480 | tf_op jit(solution)/shard_map/ppermute | solution.py:220
  278.4 19.3 %all-to-all-start = ((bf16[4,1152,128]{2,1,0:T(8,128)(2,1)}), bf16[4,1152,128]{2,1,0:T(8,128)(2,1)S(1)}, u32[]{:S(2)}, u32[]{:S(2)}) async-start(bf16[4,1152,128]{2,1,0:T(8,128)(2,1)} %pad_maximum_fusion), calls=%async_computation | async-start | bytes 2359296 | tf_op jit(solution)/shard_map/all_to_all | solution.py:225
  327.9 10.9 %all-to-all-start.3 = ((f32[32,1,1]{2,1,0:T(1,128)}), f32[32,1,1]{2,1,0:T(1,128)S(1)}, u32[]{:S(2)}, u32[]{:S(2)}) async-start(f32[32,1,1]{2,1,0:T(1,128)} %broadcast_in_dim.51), calls=%async_computation.3 | async-start | bytes 32768 | tf_op jit(solution)/shard_map/all_to_all | solution.py:32
  356.5 19.6 %all-to-all-start.5 = ((bf16[4,1152,128]{2,1,0:T(8,128)(2,1)}), bf16[4,1152,128]{2,1,0:T(8,128)(2,1)S(1)}, u32[]{:S(2)}, u32[]{:S(2)}) async-start(bf16[4,1152,128]{2,1,0:T(8,128)(2,1)} %broadcast_in_dim.54), calls=%async_computation.5 | async-start | bytes 2359296 | tf_op jit(solution)/shard_map/all_to_all | solution.py:225
  377.8 29.7 %all-to-all-start.6 = ((bf16[4,2048,128]{2,1,0:T(8,128)(2,1)}), bf16[4,2048,128]{2,1,0:T(8,128)(2,1)S(1)}, u32[]{:S(2)}, u32[]{:S(2)}) async-start(bf16[4,2048,128]{2,1,0:T(8,128)(2,1)} %broadcast_in_dim.55), calls=%async_computation.6 | async-start | bytes 4194304 | tf_op jit(solution)/shard_map/all_to_all | solution.py:225
  382.7 15.2 %collective-permute-start.28 = (bf16[2304,128]{1,0:T(8,128)(2,1)S(1)}, bf16[2304,128]{1,0:T(8,128)(2,1)S(1)}, u32[]{:S(2)}, u32[]{:S(2)}) collective-permute-start(bf16[2304,128]{1,0:T(8,128)(2,1)S(1)} %bitcast.188), channel_id=1, source_target_pairs={{12,0},{0,4},{4,8},{8,12},{13,1},{1,5},{5,9},{9,13},{14,2},{2,6},{... | collective-permute-start | bytes 1769480 | tf_op jit(solution)/shard_map/ppermute | solution.py:79
  383.1 16.7 %collective-permute-start.29 = (bf16[2304,128]{1,0:T(8,128)(2,1)S(1)}, bf16[2304,128]{1,0:T(8,128)(2,1)}, u32[]{:S(2)}, u32[]{:S(2)}) collective-permute-start(bf16[2304,128]{1,0:T(8,128)(2,1)S(1)} %bitcast.189), channel_id=1, source_target_pairs={{4,0},{8,4},{12,8},{0,12},{5,1},{9,5},{13,9},{1,13},{6,2},{10,6},{... | collective-permute-start | bytes 1769480 | tf_op jit(solution)/shard_map/ppermute | solution.py:79
  385.6 24.7 %collective-permute-start.32 = (bf16[2304,128]{1,0:T(8,128)(2,1)S(1)}, bf16[2304,128]{1,0:T(8,128)(2,1)}, u32[]{:S(2)}, u32[]{:S(2)}) collective-permute-start(bf16[2304,128]{1,0:T(8,128)(2,1)S(1)} %bitcast.184), channel_id=1, source_target_pairs={{96,0},{0,32},{32,64},{64,96},{97,1},{1,33},{33,65},{65,97},{98,2}... | collective-permute-start | bytes 1769480 | tf_op jit(solution)/shard_map/ppermute | solution.py:79
  386.7 25.0 %collective-permute-start.33 = (bf16[2304,128]{1,0:T(8,128)(2,1)S(1)}, bf16[2304,128]{1,0:T(8,128)(2,1)}, u32[]{:S(2)}, u32[]{:S(2)}) collective-permute-start(bf16[2304,128]{1,0:T(8,128)(2,1)S(1)} %bitcast.185), channel_id=1, source_target_pairs={{32,0},{64,32},{96,64},{0,96},{33,1},{65,33},{97,65},{1,97},{34,2}... | collective-permute-start | bytes 1769480 | tf_op jit(solution)/shard_map/ppermute | solution.py:79
  388.3 26.9 %collective-permute-start.39 = (bf16[2304,128]{1,0:T(8,128)(2,1)S(1)}, bf16[2304,128]{1,0:T(8,128)(2,1)}, u32[]{:S(2)}, u32[]{:S(2)}) collective-permute-start(bf16[2304,128]{1,0:T(8,128)(2,1)S(1)} %bitcast.190), channel_id=1, source_target_pairs={{0,1},{1,0},{2,3},{3,2},{4,5},{5,4},{6,7},{7,6},{8,9},{9,8},{10,11... | collective-permute-start | bytes 1769480 | tf_op jit(solution)/shard_map/ppermute | solution.py:83
  397.9 18.4 %collective-permute-start.44 = (bf16[2304,128]{1,0:T(8,128)(2,1)S(1)}, bf16[2304,128]{1,0:T(8,128)(2,1)}, u32[]{:S(2)}, u32[]{:S(2)}) collective-permute-start(bf16[2304,128]{1,0:T(8,128)(2,1)S(1)} %bitcast.186), channel_id=1, source_target_pairs={{0,1},{1,0},{2,3},{3,2},{4,5},{5,4},{6,7},{7,6},{8,9},{9,8},{10,11... | collective-permute-start | bytes 1769480 | tf_op jit(solution)/shard_map/ppermute | solution.py:83
  407.5 28.2 %collective-permute-start.49 = (bf16[8192,128]{1,0:T(8,128)(2,1)S(1)}, bf16[8192,128]{1,0:T(8,128)(2,1)S(1)}, u32[]{:S(2)}, u32[]{:S(2)}) collective-permute-start(bf16[8192,128]{1,0:T(8,128)(2,1)S(1)} %bitcast.182), channel_id=1, source_target_pairs={{0,1},{1,0},{2,3},{3,2},{4,5},{5,4},{6,7},{7,6},{8,9},{9,8},{10,11... | collective-permute-start | bytes 6291464 | tf_op jit(solution)/shard_map/ppermute | solution.py:83
  410.4 9.8 %collective-permute-start.30 = (bf16[1152,128]{1,0:T(8,128)(2,1)S(1)}, bf16[1152,128]{1,0:T(8,128)(2,1)S(1)}, u32[]{:S(2)}, u32[]{:S(2)}) collective-permute-start(bf16[1152,128]{1,0:T(8,128)(2,1)S(1)} %slice.286), channel_id=1, source_target_pairs={{12,0},{0,4},{4,8},{8,12},{13,1},{1,5},{5,9},{9,13},{14,2},{2,6},{... | collective-permute-start | bytes 884744 | tf_op jit(solution)/shard_map/ppermute | solution.py:79
  411.7 9.4 %collective-permute-start.31 = (bf16[1152,128]{1,0:T(8,128)(2,1)S(1)}, bf16[1152,128]{1,0:T(8,128)(2,1)S(1)}, u32[]{:S(2)}, u32[]{:S(2)}) collective-permute-start(bf16[1152,128]{1,0:T(8,128)(2,1)S(1)} %slice.287), channel_id=1, source_target_pairs={{4,0},{8,4},{12,8},{0,12},{5,1},{9,5},{13,9},{1,13},{6,2},{10,6},{... | collective-permute-start | bytes 884744 | tf_op jit(solution)/shard_map/ppermute | solution.py:79
  415.2 9.1 %collective-permute-start.34 = (bf16[1152,128]{1,0:T(8,128)(2,1)S(1)}, bf16[1152,128]{1,0:T(8,128)(2,1)S(1)}, u32[]{:S(2)}, u32[]{:S(2)}) collective-permute-start(bf16[1152,128]{1,0:T(8,128)(2,1)S(1)} %slice.289), channel_id=1, source_target_pairs={{96,0},{0,32},{32,64},{64,96},{97,1},{1,33},{33,65},{65,97},{98,2}... | collective-permute-start | bytes 884744 | tf_op jit(solution)/shard_map/ppermute | solution.py:79
  416.3 9.5 %collective-permute-start.35 = (bf16[1152,128]{1,0:T(8,128)(2,1)S(1)}, bf16[1152,128]{1,0:T(8,128)(2,1)S(1)}, u32[]{:S(2)}, u32[]{:S(2)}) collective-permute-start(bf16[1152,128]{1,0:T(8,128)(2,1)S(1)} %slice.290), channel_id=1, source_target_pairs={{32,0},{64,32},{96,64},{0,96},{33,1},{65,33},{97,65},{1,97},{34,2}... | collective-permute-start | bytes 884744 | tf_op jit(solution)/shard_map/ppermute | solution.py:79
  425.9 9.8 %collective-permute-start.40 = (bf16[2304,128]{1,0:T(8,128)(2,1)S(1)}, bf16[2304,128]{1,0:T(8,128)(2,1)S(1)}, u32[]{:S(2)}, u32[]{:S(2)}) collective-permute-start(bf16[2304,128]{1,0:T(8,128)(2,1)S(1)} %copy-done.1), channel_id=1, source_target_pairs={{0,1},{1,0},{2,3},{3,2},{4,5},{5,4},{6,7},{7,6},{8,9},{9,8},{10,11... | collective-permute-start | bytes 1769480 | tf_op jit(solution)/shard_map/ppermute | solution.py:83
  426.4 9.3 %collective-permute-start.41 = (bf16[2304,128]{1,0:T(8,128)(2,1)}, bf16[2304,128]{1,0:T(8,128)(2,1)S(1)}, u32[]{:S(2)}, u32[]{:S(2)}) collective-permute-start(bf16[2304,128]{1,0:T(8,128)(2,1)} %collective-permute-done.29.rest_2_), channel_id=1, source_target_pairs={{0,1},{1,0},{2,3},{3,2},{4,5},{5,4},{6,7},{7,6},{8,9},{9,8},{10,11... | collective-permute-start | bytes 1769480 | tf_op jit(solution)/shard_map/ppermute | solution.py:83
  (57 other events, 501.6 us)
